TPU v7x, 32 devices: a whole 2x2x4 slice. The times are simulated.
32 devices in a mesh: batch: 4 (over y, x), seq: 8 (over z, core).
Axes of the slice: x: 2, y: 2, z: 4, core: 2. Of those that a mesh axis runs over, the one named last changes fastest.
Arguments:
- tokens: bfloat16 [8, 1024, 768], P('batch', 'seq'), may hold values from -6 to 6
- attn_in_weight: bfloat16 [768, 2304], replicated, may hold values from -0.21875 to 0.21875
- out_weight: bfloat16 [768, 768], replicated, may hold values from -3.5 to 3.5
- ffn_in_weight: bfloat16 [768, 3072], replicated, may hold values from -0.21875 to 0.21875
- ffn_out_weight: bfloat16 [3072, 768], replicated, may hold values from -0.109375 to 0.109375
- vera_in: bfloat16 [768, 1024], replicated, may hold values from -0.21875 to 0.21875
- vera_out: bfloat16 [1024, 768], replicated, may hold values from -0.1875 to 0.1875
- rank_scale: float32 [2, 1024], replicated, may hold values from 0.3 to 1.2
- out_scale: float32 [2, 768], replicated, may hold values from -3 to 3
- gains: float32 [2, 768], replicated, may hold values from 0.25 to 1.75
- shifts: float32 [6, 768], replicated, may hold values from -2 to 2
- ffn_bias: float32 [3072], replicated, may hold values from -2 to 2
- splits: int32 [8], P('batch'), may hold values from 1 to 1023, as said below
- out_grad: bfloat16 [8, 1024, 768], P('batch', 'seq'), may hold values from -6 to 6
Outputs:
- layer_out: bfloat16 [8, 1024, 768], P('batch', 'seq')
- in_grad: bfloat16 [8, 1024, 768], P('batch', 'seq')
- rank_scale_grad: float32 [2, 1024], replicated
- out_scale_grad: float32 [2, 768], replicated
- scale_norms: float32 [4], replicated
Inputs may be any that keep to these rules, and one draw needn't show every extreme that they name: Positions below splits[s] form the first document of packed sequence s and the others the second; a token attends only within its document.
All inputs are finite; a program needn't handle non-finite values.
Results may differ from a plain program's by a relative error of at most 0.02.
Values may be sent and summed in bfloat16 or wider, within the bound.
A program may use at most 256 MiB of HBM per device.

v0:
```python
import jax
import jax.numpy as jnp
from jax import lax
from jax.sharding import PartitionSpec as P

HEADS = 12


masked_score = -1e30
key_block = 512


def product(left_side, right_side):
    return jnp.dot(left_side, right_side, preferred_element_type=jnp.float32)


def product_t(left_side, right_side):
    return lax.dot_general(
        left_side, right_side, (((1,), (1,)), ((), ())), preferred_element_type=jnp.float32
    )


def gelu_exact(inputs):
    return jax.nn.gelu(inputs, approximate=False)


def norm_forward(values_in, gain_row, shift_row):
    centered = values_in - jnp.mean(values_in, axis=-1, keepdims=True)
    inverse = lax.rsqrt(jnp.mean(centered * centered, axis=-1, keepdims=True) + 1e-05)
    normed = centered * inverse
    return (normed * gain_row + shift_row, normed, inverse)


def norm_backward(grad_in, normed, inverse, gain_row):
    scaled = grad_in * gain_row
    return inverse * (
        scaled
        - jnp.mean(scaled, axis=-1, keepdims=True)
        - normed * jnp.mean(scaled * normed, axis=-1, keepdims=True)
    )


def block_width():
    return key_block


def body(
    tokens,
    attn_in_weight,
    out_weight,
    ffn_in_weight,
    ffn_out_weight,
    vera_in,
    vera_out,
    rank_scale,
    out_scale,
    gains,
    shifts,
    ffn_bias,
    splits,
    out_grad,
):
    sequences, per_device, model_width = tokens.shape
    head_dim = model_width // HEADS
    score_scale = head_dim ** (-0.5)
    cycle_place = lax.axis_index("seq")
    token_rows = tokens.reshape(-1, model_width)
    token_float = token_rows.astype(jnp.float32)
    rank_in = product(token_rows, vera_in)
    rank_q = (rank_in * rank_scale[0]).astype(jnp.bfloat16)
    rank_v = (rank_in * rank_scale[1]).astype(jnp.bfloat16)
    wide_q = product(rank_q, vera_out)
    wide_v = product(rank_v, vera_out)
    projected = product(token_rows, attn_in_weight)
    query = projected[:, :model_width] + shifts[0] + out_scale[0] * wide_q
    keys = projected[:, model_width : 2 * model_width]
    values = projected[:, 2 * model_width :] + shifts[1] + out_scale[1] * wide_v
    query_low = query.astype(jnp.bfloat16).reshape(sequences, per_device, HEADS, head_dim)
    pair_low = (
        jnp.concatenate([keys, values], axis=-1)
        .astype(jnp.bfloat16)
        .reshape(sequences, per_device, 2 * model_width)
    )
    query_pos = cycle_place * per_device + jnp.arange(per_device, dtype=jnp.int32)
    query_side = query_pos[None, :] < splits[:, None]

    def block_scores(pair_piece, block_start):
        count_keys = pair_piece.shape[1]
        key_pos = block_start + jnp.arange(count_keys, dtype=jnp.int32)
        key_side = key_pos[None, :] < splits[:, None]
        allowed = (query_side[:, :, None] == key_side[:, None, :])[:, None]
        key_heads = pair_piece[:, :, :model_width].reshape(sequences, count_keys, HEADS, head_dim)
        value_heads = pair_piece[:, :, model_width:].reshape(sequences, count_keys, HEADS, head_dim)
        raw_scores = (
            jnp.einsum("sqhe,skhe->shqk", query_low, key_heads, preferred_element_type=jnp.float32)
            * score_scale
        )
        return (raw_scores, allowed, key_heads, value_heads)

    start_max = jnp.full((sequences, HEADS, per_device), masked_score, jnp.float32)
    start_sum = jnp.zeros((sequences, HEADS, per_device), jnp.float32)
    start_acc = jnp.zeros((sequences, per_device, HEADS, head_dim), jnp.float32)
    carry = (start_max, start_sum, start_acc)
    pair_piece = lax.all_gather(pair_low, "seq", axis=1, tiled=True)
    shard_start = jnp.int32(0)
    count_keys = pair_piece.shape[1]
    block_size = block_width()
    for absorb_block_index in range(count_keys // block_size):
        absorb_pair_piece = pair_piece[
            :, absorb_block_index * block_size : (absorb_block_index + 1) * block_size
        ]
        running_max, running_sum, absorb_accumulated = carry
        absorb_raw_scores, absorb_allowed, absorb_key_heads, absorb_value_heads = block_scores(
            absorb_pair_piece, shard_start + absorb_block_index * block_size
        )
        new_max = jnp.maximum(
            running_max,
            jnp.max(jnp.where(absorb_allowed, absorb_raw_scores, masked_score), axis=-1),
        )
        block_weights = jnp.where(
            absorb_allowed, jnp.exp(absorb_raw_scores - new_max[..., None]), 0.0
        )
        rescale = jnp.exp(running_max - new_max)
        running_sum = running_sum * rescale + jnp.sum(block_weights, axis=-1)
        added = jnp.einsum(
            "shqk,skhe->sqhe",
            block_weights.astype(jnp.bfloat16),
            absorb_value_heads,
            preferred_element_type=jnp.float32,
        )
        absorb_accumulated = (
            absorb_accumulated * jnp.transpose(rescale, (0, 2, 1))[..., None] + added
        )
        carry = (new_max, running_sum, absorb_accumulated)
    final_max, final_sum, accumulated = carry
    attended = accumulated / jnp.transpose(final_sum, (0, 2, 1))[..., None]
    log_total = final_max + jnp.log(final_sum)
    branch = product(attended.reshape(-1, model_width).astype(jnp.bfloat16), out_weight) + shifts[2]
    hidden, normed_one, inverse_one = norm_forward(token_float + branch, gains[0], shifts[4])
    inner = product(hidden.astype(jnp.bfloat16), ffn_in_weight) + ffn_bias
    activated, gelu_pull = jax.vjp(gelu_exact, inner)
    ffn_branch = product(activated.astype(jnp.bfloat16), ffn_out_weight) + shifts[3]
    layer_out, normed_two, inverse_two = norm_forward(hidden + ffn_branch, gains[1], shifts[5])
    grad_two = norm_backward(
        out_grad.reshape(-1, model_width).astype(jnp.float32), normed_two, inverse_two, gains[1]
    )
    grad_act = product_t(grad_two.astype(jnp.bfloat16), ffn_out_weight)
    grad_inner = gelu_pull(grad_act)[0].astype(jnp.bfloat16)
    grad_hidden = grad_two + product_t(grad_inner, ffn_in_weight)
    grad_one = norm_backward(grad_hidden, normed_one, inverse_one, gains[0])
    grad_att = (
        product_t(grad_one.astype(jnp.bfloat16), out_weight)
        .astype(jnp.bfloat16)
        .reshape(sequences, per_device, HEADS, head_dim)
    )
    delta = jnp.transpose(jnp.sum(grad_att.astype(jnp.float32) * attended, axis=-1), (0, 2, 1))
    grad_query = jnp.zeros((sequences, per_device, HEADS, head_dim), jnp.float32)
    whole_pairs = lax.all_gather(pair_low, "seq", axis=1, tiled=True)
    whole_len = whole_pairs.shape[1]
    block_size = block_width()
    key_terms = []
    for block_index in range(whole_len // block_size):
        block_pair_piece = whole_pairs[:, block_index * block_size : (block_index + 1) * block_size]
        block_raw_scores, block_allowed, block_key_heads, block_value_heads = block_scores(
            block_pair_piece, block_index * block_size
        )
        prob = jnp.where(block_allowed, jnp.exp(block_raw_scores - log_total[..., None]), 0.0)
        grad_prob = jnp.einsum(
            "sqhe,skhe->shqk", grad_att, block_value_heads, preferred_element_type=jnp.float32
        )
        grad_score = (prob * (grad_prob - delta[..., None])).astype(jnp.bfloat16)
        grad_value = jnp.einsum(
            "shqk,sqhe->skhe",
            prob.astype(jnp.bfloat16),
            grad_att,
            preferred_element_type=jnp.float32,
        )
        grad_key = (
            jnp.einsum("shqk,sqhe->skhe", grad_score, query_low, preferred_element_type=jnp.float32)
            * score_scale
        )
        query_part = (
            jnp.einsum(
                "shqk,skhe->sqhe", grad_score, block_key_heads, preferred_element_type=jnp.float32
            )
            * score_scale
        )
        block_count_keys = block_pair_piece.shape[1]
        pair_part = jnp.concatenate(
            [
                grad_key.reshape(sequences, block_count_keys, model_width),
                grad_value.reshape(sequences, block_count_keys, model_width),
            ],
            axis=-1,
        )
        query_part, pair_part = (query_part, pair_part)
        grad_query = grad_query + query_part
        key_terms.append(pair_part)
    pair_sum = lax.psum_scatter(
        jnp.concatenate(key_terms, axis=1), "seq", scatter_dimension=1, tiled=True
    )
    pair_grad_low = pair_sum.astype(jnp.bfloat16).reshape(-1, 2 * model_width)
    query_grad_low = grad_query.reshape(-1, model_width).astype(jnp.bfloat16)
    query_grad_float = query_grad_low.astype(jnp.float32)
    value_grad_float = pair_grad_low[:, model_width:].astype(jnp.float32)
    grad_wide_q = (query_grad_float * out_scale[0]).astype(jnp.bfloat16)
    grad_wide_v = (value_grad_float * out_scale[1]).astype(jnp.bfloat16)
    grad_rank_q = product_t(grad_wide_q, vera_out)
    grad_rank_v = product_t(grad_wide_v, vera_out)
    grad_rank_in = (grad_rank_q * rank_scale[0] + grad_rank_v * rank_scale[1]).astype(jnp.bfloat16)
    grad_tokens = (
        grad_one
        + product_t(jnp.concatenate([query_grad_low, pair_grad_low], axis=-1), attn_in_weight)
        + product_t(grad_rank_in, vera_in)
    )
    rank_terms = jnp.stack(
        [jnp.sum(grad_rank_q * rank_in, axis=0), jnp.sum(grad_rank_v * rank_in, axis=0)]
    )
    out_terms = jnp.stack(
        [jnp.sum(query_grad_float * wide_q, axis=0), jnp.sum(value_grad_float * wide_v, axis=0)]
    )
    rank_total, out_total = lax.psum((rank_terms, out_terms), ("batch", "seq"))
    scale_norms = jnp.concatenate(
        [
            jnp.sqrt(jnp.sum(rank_total * rank_total, axis=1)),
            jnp.sqrt(jnp.sum(out_total * out_total, axis=1)),
        ]
    )
    return (
        layer_out.astype(jnp.bfloat16).reshape(sequences, per_device, model_width),
        grad_tokens.astype(jnp.bfloat16).reshape(sequences, per_device, model_width),
        rank_total,
        out_total,
        scale_norms,
    )


def solution(mesh):
    in_specs = (
        P("batch", "seq", None),
        P(),
        P(),
        P(),
        P(),
        P(),
        P(),
        P(),
        P(),
        P(),
        P(),
        P(),
        P("batch"),
        P("batch", "seq", None),
    )
    out_specs = (P("batch", "seq", None), P("batch", "seq", None), P(), P(), P())
    return jax.shard_map(body, mesh=mesh, in_specs=in_specs, out_specs=out_specs, check_vma=False)
```

profile of v0, /device:TPU:12, one launch (start us, length us, event | category | flops | bytes accessed | tf_op | source)
XLA Modules:
  0.0 403.0 jit_solution(3006684528582033615)
XLA Ops:
  10.8 2.1 fusion.144
  25.8 56.0 %all-gather.2.cloned.1.call-done = bf16[2,1024,1536]{2,1,0:T(8,128)(2,1)} async-done(((bf16[2,128,1536]{2,1,0:T(8,128)(2,1)}), bf16[2,1024,1536]{2,1,0:T(8,128)(2,1)}) %all-gather.2.cloned.1.call-update) | async-done | bytes 6291472 | tf_op jit(solution)/shard_map/all_gather | solution.py:104
  81.8 5.6 %fusion.136 = (bf16[2,512,768]{2,1,0:T(8,128)(2,1)}, bf16[2,512,768]{2,1,0:T(8,128)(2,1)}, bf16[2,512,768]{2,1,0:T(8,128)(2,1)}, bf16[2,512,768]{2,1,0:T(8,128)(2,1)}) fusion(bf16[2,1024,1536]{2,1,0:T(8,128)(2,1)} %all-gather.2.cloned.1.call-done), kind=kLoop, calls=%fused_computation.202 | loop fusion | bytes 12582912 | tf_op jit(solution)/shard_map/slice | solution.py:93
  87.4 2.6 copy.36
  89.9 2.6 copy.33
  92.6 2.9 select_reduce_fusion.1
  98.2 3.7 fusion
  102.6 2.6 copy.38
  105.2 2.7 copy.35
  108.0 4.9 %fusion.53 = f32[2,128,12,64]{1,3,2,0:T(8,128)S(1)} fusion(bf16[2,512,12,64]{1,3,2,0:T(8,128)(2,1)} %bitcast.135, f32[2,12,128,512]{3,2,1,0:T(8,128)} %copy-done.1, f32[2,12,128]{2,1,0:T(8,128)} %copy-done.35, pred[2,128,512]{2,1,0:T(8,128)(4,1)} %get-tuple-element.37, f32[2,128,12]{1,2,0:T(8,128)} %get-tuple-element.30, f32[2,128,12]{1,2,0:T(8,128)} %get-tuple-element.31), kind=kOutput, calls=%fused_computation.67 | convolution fusion | flops 208011264 | bytes 8818688 | tf_op jit(solution)/shard_map/shqk,skhe->sqhe/dot_general | solution.py:125
  113.0 5.5 %fusion.138 = (bf16[2,128,12,64]{1,3,2,0:T(8,128)(2,1)S(1)}, f32[2,128,12,64]{1,3,2,0:T(8,128)}) fusion(f32[2,128,12]{1,2,0:T(8,128)S(1)} %copy-done.45, f32[2,128,12,64]{1,3,2,0:T(8,128)S(1)} %fusion.53, bf16[2,512,12,64]{1,3,2,0:T(8,128)(2,1)S(1)} %bitcast.133, f32[2,12,128,512]{3,2,1,0:T(8,128)} %copy-done.2, f32[2,12,128]{2,1,0:T(8,128)S(1)} %copy-done.34, ...), kind=kOutput, calls=%fused_computation.204 | convolution fusion | flops 208207872 | bytes 9986048 | tf_op jit(solution)/shard_map/shqk,skhe->sqhe/dot_general | solution.py:125
  121.7 8.2 %fusion.140 = (f32[256]{0:T(256)S(1)}, f32[256,768]{1,0:T(8,128)S(1)}) fusion(f32[768]{0:T(1024)S(1)} %copy-done.57, bf16[3072,768]{1,0:T(8,128)(2,1)S(1)} %bitcast.156, f32[256,3072]{1,0:T(8,128)S(1)} %convolution_add_fusion, f32[768]{0:T(1024)S(1)} %copy-done.56, f32[768]{0:T(1024)S(1)} %copy-done.55, f32[256]{0:T(256)S(1)} %add_rsqrt_fusion.1, ...), kind=kOutput, calls=%fused_computation.206 | convolution fusion | flops 1260453632 | bytes 9449472 | tf_op jit(solution)/shard_map/dot_general | solution.py:14
  131.8 15.9 %fusion.135 = (f32[256]{0:T(256)}, f32[256]{0:T(256)}, f32[256,768]{1,0:T(8,128)}) fusion(f32[256]{0:T(256)} %copy-done.49, f32[256,768]{1,0:T(8,128)} %copy-done.19, f32[256]{0:T(256)} %copy-done.46, f32[768]{0:T(1024)} %get-tuple-element.16, f32[256,768]{1,0:T(8,128)} %get-tuple-element.27, bf16[768,3072]{1,0:T(8,128)(2,1)} %param.17, ...), kind=kOutput, calls=%fused_computation.201 | convolution fusion | flops 2474114560 | bytes 14949376 | tf_op jit(solution)/shard_map/dot_general | solution.py:18
  149.7 3.1 convolution_convert_fusion
  152.8 2.0 copy.40
  158.4 5.9 %fusion.7 = f32[2,12,64,512]{3,2,1,0:T(8,128)} fusion(f32[2,12,128,512]{3,2,1,0:T(8,128)} %copy-done.2, f32[2,12,128]{2,1,0:T(8,128)S(1)} %log_add_fusion, pred[2,128,512]{2,1,0:T(8,128)(4,1)} %get-tuple-element.36, bf16[2,128,12,64]{1,0,3,2:T(2,128)(2,1)} %reshape.231), kind=kOutput, calls=%fused_computation.18 | convolution fusion | flops 207618048 | bytes 9973760 | tf_op jit(solution)/shard_map/shqk,sqhe->skhe/dot_general | solution.py:172
  164.3 5.5 %multiply_convert_fusion = bf16[2,12,128,512]{3,2,1,0:T(8,128)(2,1)} fusion(f32[2,12,128,512]{3,2,1,0:T(8,128)} %copy-done.2, f32[2,12,128]{2,1,0:T(8,128)S(1)} %bitcast.151, f32[2,12,128]{2,1,0:T(8,128)S(1)} %log_add_fusion, pred[2,128,512]{2,1,0:T(8,128)(4,1)S(1)} %copy-done.24, bf16[2,512,12,64]{1,3,2,0:T(8,128)(2,1)S(1)} %bitcast.134, ...), kind=kOutput, calls=%fused_computation.1 | convolution fusion | flops 210763776 | bytes 11558912 | tf_op jit(solution)/shard_map/sqhe,skhe->shqk/dot_general | solution.py:168
  169.9 3.6 multiply_convert_fusion.1
  173.5 2.7 fusion.9
  176.2 3.6 copy.52
  179.7 4.4 %convolution_multiply_fusion = f32[2,12,64,512]{3,2,1,0:T(8,128)} fusion(bf16[2,12,128,512]{3,2,1,0:T(8,128)(2,1)} %multiply_convert_fusion, bf16[2,128,12,64]{1,0,3,2:T(2,128)(2,1)} %reshape.225), kind=kOutput, calls=%fused_computation.53 | convolution fusion | flops 202113024 | bytes 6684672 | tf_op jit(solution)/shard_map/shqk,sqhe->skhe/dot_general | solution.py:179
  184.2 2.3 convolution_multiply_fusion.1
  186.4 3.5 copy.47
  190.0 3.6 copy.51
  193.6 3.6 copy.48
  197.2 13.0 %maximum_maximum_fusion = f32[2,1024,1536]{2,1,0:T(8,128)} fusion(f32[2,512,768]{2,1,0:T(8,128)} %copy.52, f32[2,512,768]{2,1,0:T(8,128)} %copy.51, f32[2,512,768]{2,1,0:T(8,128)} %copy.48, f32[2,512,768]{2,1,0:T(8,128)} %copy.47), kind=kLoop, calls=%fused_computation | loop fusion | flops 9437184 | bytes 25165824 | tf_op jit(solution)/shard_map/concatenate | solution.py:200
  210.2 3.7 fusion.145
  216.5 2.0 copy.53
  219.9 117.7 %reduce-scatter.2.cloned.1.call-done = f32[2,128,1536]{2,1,0:T(8,128)} async-done(((f32[2,1024,1536]{2,1,0:T(8,128)}), f32[2,128,1536]{2,1,0:T(8,128)}) %reduce-scatter.2.cloned.1.call-update) | async-done | bytes 1572880 | tf_op jit(solution)/shard_map/reduce_scatter | solution.py:199
  339.2 3.7 convolution_add_fusion.4
  346.5 43.6 %all-reduce = (f32[2,1024]{1,0:T(2,128)}, f32[2,768]{1,0:T(2,128)}) all-reduce(f32[2,1024]{1,0:T(2,128)S(1)} %pad_maximum_fusion.1, f32[2,768]{1,0:T(2,128)} %pad_maximum_fusion.2), channel_id=1, replica_groups=mesh['batch'=4,'seq'=8] {'batch','seq'}, use_global_device_ids=true, to_apply=%region_16.17 | all-reduce | flops 3584 | bytes 28672 | tf_op jit(solution)/shard_map/psum | solution.py:222
  391.8 3.6 fusion.60
  (198 shorter events, 41.3 us)
Async XLA Ops:
  7.2 5.7 %copy-start = (bf16[768,2304]{1,0:T(8,128)(2,1)S(1)}, bf16[768,2304]{1,0:T(8,128)(2,1)}, u32[]{:S(2)}) copy-start(bf16[768,2304]{1,0:T(8,128)(2,1)} %param.15) | copy-start | bytes 10616836
  7.2 74.6 %all-gather.2.cloned.1.call-start = ((), (), s32[]{:S(2)}) async-start(), calls=%async_computation.1 | async-start | bytes 7077888 | tf_op jit(solution)/shard_map/all_gather | solution.py:104
  7.2 5.7 %copy-start.28 = (bf16[2,128,768]{2,1,0:T(8,128)(2,1)S(1)}, bf16[2,128,768]{2,1,0:T(8,128)(2,1)}, u32[]{:S(2)}) copy-start(bf16[2,128,768]{2,1,0:T(8,128)(2,1)} %param.14) | copy-start | bytes 1179652
  8.1 6.0 %copy-start.40 = (f32[1,1024]{1,0:T(1,128)}, f32[1,1024]{1,0:T(1,128)S(1)}, u32[]{:S(2)}) copy-start(f32[1,1024]{1,0:T(1,128)S(1)} %get-tuple-element.35) | copy-start | bytes 12292
  8.1 7.2 %copy-start.38 = (f32[1,1024]{1,0:T(1,128)}, f32[1,1024]{1,0:T(1,128)S(1)}, u32[]{:S(2)}) copy-start(f32[1,1024]{1,0:T(1,128)S(1)} %get-tuple-element.34) | copy-start | bytes 12292
  9.1 6.2 %copy-start.36 = (f32[768]{0:T(1024)}, f32[768]{0:T(1024)S(1)}, u32[]{:S(2)}) copy-start(f32[768]{0:T(1024)S(1)} %get-tuple-element.18) | copy-start | bytes 9220
  9.1 6.2 %copy-start.42 = (f32[768]{0:T(1024)}, f32[768]{0:T(1024)S(1)}, u32[]{:S(2)}) copy-start(f32[768]{0:T(1024)S(1)} %get-tuple-element.17) | copy-start | bytes 9220
  17.0 7.1 %copy-start.59 = (s32[2]{0:T(128)S(1)}, s32[2]{0:T(128)}, u32[]{:S(2)}) copy-start(s32[2]{0:T(128)} %param.26) | copy-start | bytes 28
  17.9 319.7 %reduce-scatter.2.cloned.1.call-start = ((), (), s32[]{:S(2)}) async-start(), calls=%async_computation.2 | async-start | bytes 14155776 | tf_op jit(solution)/shard_map/reduce_scatter | solution.py:199
  96.9 5.0 %copy-start.2 = (f32[2,12,128,512]{3,2,1,0:T(8,128)}, f32[2,12,128,512]{3,2,1,0:T(8,128)S(1)}, u32[]{:S(2)}) copy-start(f32[2,12,128,512]{3,2,1,0:T(8,128)S(1)} %get-tuple-element.42) | copy-start | bytes 18874372
  112.9 6.9 %slice-start.4 = ((s8[4718592]{0:T(1024)(128)(4,1)}), s8[4194304]{0:T(1024)(128)(4,1)S(1)}, s32[]{:S(2)}) async-start(s8[4718592]{0:T(1024)(128)(4,1)} %bitcast.157), calls=%async_computation.7 | async-start | bytes 8388608
  113.0 5.9 %copy-start.29 = (bf16[2,128,768]{2,1,0:T(8,128)(2,1)S(1)}, bf16[2,128,768]{2,1,0:T(8,128)(2,1)}, u32[]{:S(2)}) copy-start(bf16[2,128,768]{2,1,0:T(8,128)(2,1)} %param.14) | copy-start | bytes 1179652
  113.0 5.9 %copy-start.30 = (bf16[768,768]{1,0:T(8,128)(2,1)S(1)}, bf16[768,768]{1,0:T(8,128)(2,1)}, u32[]{:S(2)}) copy-start(bf16[768,768]{1,0:T(8,128)(2,1)} %param.16) | copy-start | bytes 3538948
  113.0 5.9 %copy-start.58 = (f32[768]{0:T(1024)S(1)}, f32[768]{0:T(1024)}, u32[]{:S(2)}) copy-start(f32[768]{0:T(1024)} %get-tuple-element.11) | copy-start | bytes 9220
  113.0 6.8 %slice-start.5 = ((s8[4718592]{0:T(1024)(128)(4,1)}), s8[524288]{0:T(1024)(128)(4,1)S(1)}, s32[]{:S(2)}) async-start(s8[4718592]{0:T(1024)(128)(4,1)} %bitcast.157), calls=%async_computation.8 | async-start | bytes 1048576
  121.4 8.5 %copy-start.61 = (f32[256,3072]{1,0:T(8,128)}, f32[256,3072]{1,0:T(8,128)S(1)}, u32[]{:S(2)}) copy-start(f32[256,3072]{1,0:T(8,128)S(1)} %convolution_add_fusion) | copy-start | bytes 9437188
  121.7 8.4 %copy-start.17 = (bf16[2,128,768]{2,1,0:T(8,128)(2,1)S(1)}, bf16[2,128,768]{2,1,0:T(8,128)(2,1)}, u32[]{:S(2)}) copy-start(bf16[2,128,768]{2,1,0:T(8,128)(2,1)} %param.27) | copy-start | bytes 1179652
  121.7 8.4 %copy-start.32 = (f32[768]{0:T(1024)S(1)}, f32[768]{0:T(1024)}, u32[]{:S(2)}) copy-start(f32[768]{0:T(1024)} %copy-done.31) | copy-start | bytes 9220
  121.7 8.8 %copy-start.44 = (f32[768]{0:T(1024)S(1)}, f32[768]{0:T(1024)}, u32[]{:S(2)}) copy-start(f32[768]{0:T(1024)} %get-tuple-element.9) | copy-start | bytes 9220
  121.7 8.8 %copy-start.51 = (f32[256]{0:T(256)S(1)}, f32[256]{0:T(256)}, u32[]{:S(2)}) copy-start(f32[256]{0:T(256)} %multiply_bitcast_fusion) | copy-start | bytes 3076
  158.3 6.0 %copy-start.16 = (bf16[2,128,12,64]{1,0,3,2:T(2,128)(2,1)S(1)}, bf16[2,128,12,64]{1,0,3,2:T(2,128)(2,1)}, u32[]{:S(2)}) copy-start(bf16[2,128,12,64]{1,0,3,2:T(2,128)(2,1)} %reshape.231) | copy-start | bytes 1179652
  158.3 6.0 %copy-start.24 = (pred[2,128,512]{2,1,0:T(8,128)(4,1)S(1)}, pred[2,128,512]{2,1,0:T(8,128)(4,1)}, u32[]{:S(2)}) copy-start(pred[2,128,512]{2,1,0:T(8,128)(4,1)} %get-tuple-element.36) | copy-start | bytes 393220
  158.3 5.9 %copy-start.26 = (bf16[2,512,768]{1,2,0:T(8,128)(2,1)S(1)}, bf16[2,512,768]{1,2,0:T(8,128)(2,1)}, u32[]{:S(2)}) copy-start(bf16[2,512,768]{1,2,0:T(8,128)(2,1)} %copy.38) | copy-start | bytes 4718596
  158.4 11.5 %slice-start = ((s8[6291456]{0:T(1024)(128)(4,1)}), s8[4194304]{0:T(1024)(128)(4,1)S(1)}, s32[]{:S(2)}) async-start(s8[6291456]{0:T(1024)(128)(4,1)} %bitcast.120), calls=%async_computation.3 | async-start | bytes 8388608
  164.3 5.5 %slice-start.1 = ((s8[6291456]{0:T(1024)(128)(4,1)}), s8[2097152]{0:T(1024)(128)(4,1)S(1)}, s32[]{:S(2)}) async-start(s8[6291456]{0:T(1024)(128)(4,1)} %bitcast.120), calls=%async_computation.4 | async-start | bytes 4194304
  164.3 5.5 %copy-start.21 = (pred[2,128,512]{2,1,0:T(8,128)(4,1)S(1)}, pred[2,128,512]{2,1,0:T(8,128)(4,1)}, u32[]{:S(2)}) copy-start(pred[2,128,512]{2,1,0:T(8,128)(4,1)} %get-tuple-element.37) | copy-start | bytes 393220
  164.3 5.5 %copy-start.27 = (bf16[2,512,768]{1,2,0:T(8,128)(2,1)S(1)}, bf16[2,512,768]{1,2,0:T(8,128)(2,1)}, u32[]{:S(2)}) copy-start(bf16[2,512,768]{1,2,0:T(8,128)(2,1)} %copy.35) | copy-start | bytes 4718596
  215.2 123.9 %copy-start.47 = (f32[256]{0:T(256)S(1)}, f32[256]{0:T(256)}, u32[]{:S(2)}) copy-start(f32[256]{0:T(256)} %copy-done.46) | copy-start | bytes 3076
  215.2 123.9 %copy-start.50 = (f32[256]{0:T(256)S(1)}, f32[256]{0:T(256)}, u32[]{:S(2)}) copy-start(f32[256]{0:T(256)} %copy-done.49) | copy-start | bytes 3076
  215.2 123.9 %copy-start.53 = (f32[256]{0:T(256)S(1)}, f32[256]{0:T(256)}, u32[]{:S(2)}) copy-start(f32[256]{0:T(256)} %copy-done.52) | copy-start | bytes 3076
  343.6 48.1 %copy-start.39 = (f32[1,1024]{1,0:T(1,128)S(1)}, f32[1,1024]{1,0:T(1,128)}, u32[]{:S(2)}) copy-start(f32[1,1024]{1,0:T(1,128)} %copy-done.38) | copy-start | bytes 12292
  343.6 48.1 %copy-start.41 = (f32[1,1024]{1,0:T(1,128)S(1)}, f32[1,1024]{1,0:T(1,128)}, u32[]{:S(2)}) copy-start(f32[1,1024]{1,0:T(1,128)} %copy-done.40) | copy-start | bytes 12292
  (38 other events, 105.8 us)
Sparse Core Ops, SparseCore 0:
  18.1 63.6 all-gather.1
  210.3 127.2 reduce-scatter.1
where the time goes:
time: 411 us; the launch traced here: 403 us
  waiting for transfers between devices  174 us (42%)
  matrix products  88.2 us (21%)
  local copies, waits for them, and re-layouts  49.9 us (12%)
  blocking collectives  43.6 us (11%)
  other arithmetic  32.2 us (8%)
  between operations  15.2 us (4%)
    reduce_scatter x1, waiting for transfers between devices, body(): lax.psum_scatter(jnp.concatenate(key_terms, axis=1), 'seq', scatter_dimen...  118 us
    all_gather x1, waiting for transfers between devices, body(): pair_piece = lax.all_gather(pair_low, 'seq', axis=1, tiled=True)  56 us
    psum x1, blocking collectives, body(): rank_total, out_total = lax.psum((rank_terms, out_terms), ('batch', 'seq'))  43.6 us
    dot_general x6, matrix products, product_t(): lax.dot_general(left_side, right_side, (((1,), (1,)), ((), ())), preferre...  28.6 us
    dot_general x7, matrix products, product(): return jnp.dot(left_side, right_side, preferred_element_type=jnp.float32)  15.7 us
    concatenate x1, other arithmetic, body(): jnp.concatenate(key_terms, axis=1)  13 us
    slice x3, local copies, waits for them, and re-layouts, block_scores(): pair_piece[:, :, model_width:]  10.9 us
    dot_general x2, matrix products, body(): jnp.einsum('shqk,skhe->sqhe', block_weights.astype(jnp.bfloat16), absorb_...  10.4 us
  transfers between devices with their start and end apart: 2, of which 2 were waited for; matrix products, arithmetic and copies ran while one was open for 4% of the time, Pallas kernels for 0%

commit v1 on v0

--- a/solution.py
+++ b/solution.py
@@ -1,6 +1,10 @@
+import functools
+
 import jax
 import jax.numpy as jnp
 from jax import lax
+from jax.experimental import pallas as pl
+from jax.experimental.pallas import tpu as pltpu
 from jax.sharding import PartitionSpec as P
 
 HEADS = 12
@@ -235,7 +239,593 @@
     )
 
 
+MESH = pl.DeviceIdType.MESH
+BIG = 1e30
+F32 = jnp.float32
+BF16 = jnp.bfloat16
+
+
+def fits(mesh):
+    return mesh.shape["seq"] == 8 and mesh.shape["batch"] == 4
+
+
+def dot(left, right):
+    return lax.dot_general(left, right, (((1,), (0,)), ((), ())), preferred_element_type=F32)
+
+
+def dot_nt(left, right):
+    return lax.dot_general(left, right, (((1,), (1,)), ((), ())), preferred_element_type=F32)
+
+
+OWN, FAR, SIB, SIB_FAR, NEAR, NEAR_FAR, SIB_NEAR, SIB_NEAR_FAR = range(8)
+
+
+def layer_kernel(
+    n_batch,
+    tokens,
+    attn_in,
+    out_w,
+    ffn_in,
+    ffn_out,
+    vera_in,
+    vera_out,
+    out_grad,
+    rank_scale,
+    out_scale,
+    gains,
+    shifts,
+    ffn_bias,
+    splits,
+    layer_out,
+    in_grad,
+    rank_total,
+    out_total,
+    tok,
+    og,
+    w_all,
+    w_out,
+    w_one,
+    w_two,
+    v_in,
+    v_out,
+    v_out_t,
+    k_ext,
+    q_ext,
+    val,
+    k_t,
+    v_t,
+    probs,
+    s_buf,
+    att_t,
+    inv_l,
+    att_send,
+    att_recv,
+    hid,
+    n_one,
+    acc,
+    gprime,
+    low_rows,
+    g_two,
+    g_one,
+    lo_buf,
+    ga_send,
+    ga_recv,
+    ga_mine,
+    go_t,
+    go_m,
+    delta,
+    d_kv,
+    dq_t,
+    ta_send,
+    ta_recv,
+    ta_mine,
+    tn_send,
+    tn_recv,
+    tb_send,
+    tb_recv,
+    ig_buf,
+    sum_buf,
+    sum_recv,
+    send_sem,
+    recv_sem,
+    load_sem,
+):
+    s = lax.axis_index("seq")
+    b = lax.axis_index("batch")
+    core = s % 2
+    group = s // 4
+    sib = s + 1 - 2 * core
+    near = s + 2 - 4 * ((s // 2) % 2)
+    far = s + 4 - 8 * group
+    bx = b + 1 - 2 * (b % 2)
+    by = b + 2 - 4 * (b // 2)
+    half = pl.multiple_of(core * 384, 384)
+    other_half = pl.multiple_of(384 - core * 384, 384)
+
+    def remote(k, src, dst, where):
+        return pltpu.make_async_remote_copy(
+            src_ref=src,
+            dst_ref=dst,
+            send_sem=send_sem.at[k],
+            recv_sem=recv_sem.at[k],
+            device_id=where,
+            device_id_type=MESH,
+        )
+
+    def local(k, src, dst):
+        return pltpu.make_async_copy(src, dst, load_sem.at[k])
+
+    def block(ref, k, n=1):
+        return ref.at[pl.ds(128 * k, 128 * n)]
+
+    to_sib, to_near, to_far = {"seq": sib}, {"seq": near}, {"seq": far}
+
+    loads = [
+        local(0, tokens.at[group], block(tok, OWN)),
+        local(1, vera_in, v_in),
+        local(2, vera_out.at[:, pl.ds(half, 384)], v_out),
+        local(3, attn_in.at[:, pl.ds(half, 384)], w_all.at[:, pl.ds(0, 384)]),
+        local(4, attn_in.at[:, pl.ds(768 + half, 384)], w_all.at[:, pl.ds(384, 384)]),
+        local(5, attn_in.at[:, pl.ds(1536 + half, 384)], w_all.at[:, pl.ds(768, 384)]),
+        local(6, out_w, w_out),
+        local(7, ffn_in, w_one),
+        local(8, ffn_out, w_two),
+        local(9, out_grad.at[group], block(og, OWN)),
+    ]
+    for item in loads:
+        item.start()
+
+    barrier = pltpu.get_barrier_semaphore()
+    for where in (to_sib, to_near, to_far, {"batch": bx}, {"batch": by}):
+        pl.semaphore_signal(barrier, inc=1, device_id=where, device_id_type=MESH)
+    pl.semaphore_wait(barrier, 5)
+
+    send_far = remote(0, tokens.at[1 - group], block(tok, FAR), to_far)
+    send_near = remote(1, tokens.at[group], block(tok, NEAR), to_near)
+    send_sib = remote(2, tokens.at[group], block(tok, SIB), to_sib)
+    pass_far_sib = remote(3, block(tok, FAR), block(tok, SIB_FAR), to_sib)
+    pass_far_near = remote(4, block(tok, FAR), block(tok, NEAR_FAR), to_near)
+    pass_near_sib = remote(5, block(tok, NEAR), block(tok, SIB_NEAR), to_sib)
+    pass_last = remote(6, block(tok, NEAR_FAR), block(tok, SIB_NEAR_FAR), to_sib)
+    send_og = remote(7, out_grad.at[1 - group], block(og, FAR), to_far)
+    send_far.start()
+    send_near.start()
+    send_sib.start()
+
+    for k in range(1, 6):
+        loads[k].wait()
+    for row, at in ((0, 0), (1, 768)):
+        scale_row = rank_scale[pl.ds(row, 1), :]
+        out_row = out_scale[pl.ds(row, 1), pl.ds(half, 384)]
+
+        def effective(t, _, at=at, scale_row=scale_row, out_row=out_row):
+            rows = pl.ds(pl.multiple_of(t * 256, 256), 256)
+            scaled = (v_in[rows, :].astype(F32) * scale_row).astype(BF16)
+            wide = dot(scaled, v_out[...]) * out_row
+            w_all[rows, at : at + 384] = (w_all[rows, at : at + 384].astype(F32) + wide).astype(BF16)
+            return 0
+
+        lax.fori_loop(0, 3, effective, 0)
+    v_out_t[...] = v_out[...].astype(F32).T.astype(BF16)
+
+    split = splits[group]
+    lane = lax.broadcasted_iota(jnp.int32, (128, 128), 1)
+    row_at = lax.broadcasted_iota(jnp.int32, (128, 128), 0)
+    flip_one, flip_two, flip_four = sib - s, near - s, far - s
+    starts = [
+        s,
+        s + flip_four,
+        s + flip_one,
+        s + flip_four + flip_one,
+        s + flip_two,
+        s + flip_two + flip_four,
+        s + flip_two + flip_one,
+        s + flip_two + flip_four + flip_one,
+    ]
+    for k in range(8):
+        first = (starts[k] * 128 + row_at < split).astype(F32)
+        second = 1.0 - first
+        key_side = jnp.where(lane == 0, first, jnp.where(lane == 1, second, 0.0)).astype(BF16)
+        for p in range(3):
+            k_ext[p, 128 * k : 128 * k + 128, 128:256] = key_side
+        if k < 4:
+            query_side = (
+                jnp.where(lane == 0, second, jnp.where(lane == 1, first, 0.0)) * (-BIG)
+            ).astype(BF16)
+            for h in range(6):
+                q_ext[h, 128 * k : 128 * k + 128, 128:256] = query_side
+
+    shift_q = shifts[0:1, pl.ds(half, 384)]
+    shift_v = shifts[1:2, pl.ds(half, 384)]
+    low_lane = lax.broadcasted_iota(jnp.int32, (256, 128), 1) < 64
+
+    def project(one, two, queries):
+        rows = jnp.concatenate(
+            [tok[128 * one : 128 * one + 128, :], tok[128 * two : 128 * two + 128, :]], axis=0
+        )
+        keys = dot(rows, w_all[:, 384:768])
+        values = dot(rows, w_all[:, 768:1152]) + shift_v
+        low_keys = keys.astype(BF16)
+        low_values = values.astype(BF16)
+        keys_t = keys.T.astype(BF16)
+        values_t = values.T.astype(BF16)
+        for n, k in ((0, one), (1, two)):
+            part = slice(128 * n, 128 * n + 128)
+            to = slice(128 * k, 128 * k + 128)
+            for p in range(3):
+                k_ext[p, to, 0:128] = low_keys[part, 128 * p : 128 * p + 128]
+                val[p, to, :] = low_values[part, 128 * p : 128 * p + 128]
+            k_t[:, to] = keys_t[:, part]
+            v_t[:, to] = values_t[:, part]
+        if queries:
+            query = dot(rows, w_all[:, 0:384]) + shift_q
+            low_query = query.astype(BF16).astype(F32) * 0.125
+            for h in range(6):
+                p = h // 2
+                mine = low_lane if h % 2 == 0 else jnp.logical_not(low_lane)
+                masked = jnp.where(mine, low_query[:, 128 * p : 128 * p + 128], 0.0).astype(BF16)
+                for n, k in ((0, one), (1, two)):
+                    q_ext[h, 128 * k : 128 * k + 128, 0:128] = masked[128 * n : 128 * n + 128]
+
+    loads[0].wait()
+    send_sib.wait_recv()
+    project(OWN, SIB, True)
+    send_near.wait_recv()
+    pass_near_sib.start()
+    send_far.wait_recv()
+    pass_far_near.start()
+    pass_far_sib.start()
+    pass_near_sib.wait_recv()
+    project(NEAR, SIB_NEAR, False)
+    pass_far_sib.wait_recv()
+    project(FAR, SIB_FAR, True)
+    pass_far_near.wait_recv()
+    pass_last.start()
+    send_og.start()
+    pass_last.wait_recv()
+    project(NEAR_FAR, SIB_NEAR_FAR, False)
+
+    def forward_head(h, _):
+        p = h // 2
+        rows_h = pl.ds(pl.multiple_of(h * 64, 64), 64)
+        top = None
+        for k in range(4):
+            part = dot_nt(k_ext[p, 256 * k : 256 * k + 256, :], q_ext[h])
+            s_buf[256 * k : 256 * k + 256, :] = part
+            peak = jnp.max(part, axis=0, keepdims=True)
+            top = peak if top is None else jnp.maximum(top, peak)
+        total = jnp.zeros((1, 512), F32)
+        out = jnp.zeros((64, 512), F32)
+        for k in range(4):
+            weight = jnp.exp(s_buf[256 * k : 256 * k + 256, :] - top)
+            total = total + jnp.sum(weight, axis=0, keepdims=True)
+            low_weight = weight.astype(BF16)
+            probs[h, 256 * k : 256 * k + 256, :] = low_weight
+            out = out + dot(v_t[rows_h, 256 * k : 256 * k + 256], low_weight)
+        inverse = 1.0 / total
+        inv_l[h] = inverse
+        att_t[rows_h, :] = out * inverse
+        return 0
+
+    lax.fori_loop(0, 6, forward_head, 0)
+
+    swap_att = remote(8, att_send, att_recv, to_sib)
+    att_send[...] = att_t[:, 256:512].T.astype(BF16)
+    swap_att.start()
+
+    def norm(values_in):
+        centered = values_in - jnp.mean(values_in, axis=-1, keepdims=True)
+        inverse = lax.rsqrt(jnp.mean(centered * centered, axis=-1, keepdims=True) + 1e-05)
+        return centered * inverse, inverse
+
+    def norm_back(grad_in, normed, inverse, gain_row):
+        scaled = grad_in * gain_row
+        return inverse * (
+            scaled
+            - jnp.mean(scaled, axis=-1, keepdims=True)
+            - normed * jnp.mean(scaled * normed, axis=-1, keepdims=True)
+        )
+
+    loads[6].wait()
+    branch = dot(att_t[:, 0:256].T.astype(BF16), w_out[pl.ds(half, 384), :])
+    swap_att.wait_recv()
+    branch = branch + dot(att_recv[...], w_out[pl.ds(other_half, 384), :]) + shifts[2:3, :]
+    normed_one, inverse_one = norm(tok[0:256, :].astype(F32) + branch)
+    n_one[...] = normed_one
+    hidden = normed_one * gains[0:1, :] + shifts[4:5, :]
+    hid[...] = hidden
+    low_rows[...] = hidden.astype(BF16)
+
+    loads[7].wait()
+    loads[8].wait()
+    acc[...] = jnp.zeros_like(acc)
+
+    def ffn_forward(t, _):
+        cols = pl.ds(pl.multiple_of(t * 512, 512), 512)
+        inner = dot(low_rows[...], w_one[:, cols]) + ffn_bias[:, cols]
+        phi = 0.5 * (1.0 + lax.erf(inner * 0.7071067811865476))
+        density = 0.3989422804014327 * jnp.exp(-0.5 * inner * inner)
+        gprime[:, cols] = phi + inner * density
+        acc[...] += dot((inner * phi).astype(BF16), w_two[cols, :])
+        return 0
+
+    lax.fori_loop(0, 6, ffn_forward, 0)
+    normed_two, inverse_two = norm(hid[...] + acc[...] + shifts[3:4, :])
+    lo_buf[...] = (normed_two * gains[1:2, :] + shifts[5:6, :]).astype(BF16)
+    send_lo = remote(10, block(lo_buf, FAR), layer_out.at[group], to_far)
+    keep_lo = local(10, block(lo_buf, OWN), layer_out.at[group])
+    send_lo.start()
+    keep_lo.start()
+    loads[9].wait()
+    send_og.wait_recv()
+    grad_two = norm_back(og[...].astype(F32), normed_two, inverse_two, gains[1:2, :])
+    g_two[...] = grad_two
+    low_rows[...] = grad_two.astype(BF16)
+    acc[...] = grad_two
+
+    def ffn_backward(t, _):
+        cols = pl.ds(pl.multiple_of(t * 512, 512), 512)
+        grad_act = dot_nt(low_rows[...], w_two[cols, :])
+        grad_inner = (grad_act * gprime[:, cols]).astype(BF16)
+        acc[...] += dot_nt(grad_inner, w_one[:, cols])
+        return 0
+
+    lax.fori_loop(0, 6, ffn_backward, 0)
+    grad_one = norm_back(acc[...], n_one[...], inverse_one, gains[0:1, :])
+    g_one[...] = grad_one
+    low_one = grad_one.astype(BF16)
+    swap_ga = remote(9, ga_send, ga_recv, to_sib)
+    ga_send[...] = dot_nt(low_one, w_out[pl.ds(other_half, 384), :]).astype(BF16)
+    swap_ga.start()
+    ga_mine[...] = dot_nt(low_one, w_out[pl.ds(half, 384), :]).astype(BF16)
+    swap_ga.wait_recv()
+
+    go_full = jnp.concatenate([ga_mine[...], ga_recv[...]], axis=0).astype(F32).T
+    top_rows = lax.broadcasted_iota(jnp.int32, (128, 512), 0) < 64
+    for p in range(3):
+        pair = go_full[128 * p : 128 * p + 128, :]
+        attended = att_t[128 * p : 128 * p + 128, :]
+        for e in range(2):
+            h = 2 * p + e
+            mine = top_rows if e == 0 else jnp.logical_not(top_rows)
+            scaled = jnp.where(mine, pair * inv_l[h], 0.0)
+            low_scaled = scaled.astype(BF16)
+            rounded = low_scaled.astype(F32)
+            go_t[h] = low_scaled
+            go_m[h] = rounded.T.astype(BF16)
+            delta[h] = jnp.sum(rounded * attended, axis=0, keepdims=True)
+
+    def backward_pair(p, start, first):
+        rows = slice(start, start + 512)
+        grad_keys = None
+        grad_values = None
+        for e in range(2):
+            h = 2 * p + e
+            rows_h = pl.ds(pl.multiple_of(h * 64, 64), 64)
+            weight = probs[h, rows, :]
+            grad_prob = dot(val[p, rows, :], go_t[h])
+            grad_score = (weight.astype(F32) * (grad_prob - delta[h])).astype(BF16)
+            value_part = dot(weight, go_m[h])
+            key_part = dot(grad_score, q_ext[h, :, 0:128])
+            query_part = dot(k_t[rows_h, rows], grad_score)
+            grad_values = value_part if e == 0 else grad_values + value_part
+            grad_keys = key_part if e == 0 else grad_keys + key_part
+            if first:
+                dq_t[rows_h, :] = query_part
+            else:
+                dq_t[rows_h, :] += query_part
+        d_kv[rows, pl.ds(pl.multiple_of(p * 128, 128), 128)] = grad_keys.astype(BF16)
+        d_kv[rows, pl.ds(pl.multiple_of(384 + p * 128, 128), 128)] = grad_values.astype(BF16)
+
+    def near_pair(p, _):
+        backward_pair(p, 512, True)
+        return 0
+
+    def own_pair(p, _):
+        backward_pair(p, 0, False)
+        return 0
+
+    lax.fori_loop(0, 3, near_pair, 0)
+    swap_ta = remote(11, ta_send, ta_recv, to_sib)
+    ta_send[...] = dot_nt(d_kv[768:1024, :], w_all[:, 384:1152]).astype(BF16)
+    swap_ta.start()
+    ta_mine[...] = dot_nt(d_kv[512:768, :], w_all[:, 384:1152])
+    lax.fori_loop(0, 1, own_pair, 0)
+    swap_ta.wait_recv()
+    tn_send[...] = (ta_mine[...] + ta_recv[...].astype(F32)).astype(BF16)
+    send_tn_far = remote(12, tn_send.at[pl.ds(128, 128)], tn_recv.at[pl.ds(128, 128)], to_near)
+    send_tn_own = remote(13, tn_send.at[pl.ds(0, 128)], tn_recv.at[pl.ds(0, 128)], to_near)
+    send_tn_far.start()
+    send_tn_own.start()
+    lax.fori_loop(1, 3, own_pair, 0)
+
+    low_dq_t = (dq_t[...] * 0.125).astype(BF16)
+    low_dq = (dq_t[...] * 0.125).T.astype(BF16)
+    swap_tb = remote(14, tb_send, tb_recv, to_sib)
+    tb_send[...] = (
+        dot_nt(d_kv[256:512, :], w_all[:, 384:1152]) + dot_nt(low_dq[256:512, :], w_all[:, 0:384])
+    ).astype(BF16)
+    swap_tb.start()
+    mine = (
+        g_one[...]
+        + dot_nt(d_kv[0:256, :], w_all[:, 384:1152])
+        + dot_nt(low_dq[0:256, :], w_all[:, 0:384])
+    )
+    swap_tb.wait_recv()
+    send_tn_far.wait_recv()
+    mine = mine + tb_recv[...].astype(F32)
+    ig_buf[128:256, :] = (mine[128:256] + tn_recv[128:256, :].astype(F32)).astype(BF16)
+    send_ig = remote(15, block(ig_buf, FAR), in_grad.at[group], to_far)
+    keep_ig = local(11, block(ig_buf, OWN), in_grad.at[group])
+    send_ig.start()
+    send_tn_own.wait_recv()
+    ig_buf[0:128, :] = (mine[0:128] + tn_recv[0:128, :].astype(F32)).astype(BF16)
+    keep_ig.start()
+
+    grad_q_map = dot(low_dq_t, tok[0:512, :]).astype(BF16)
+    grad_v_map = dot(d_kv[:, 384:768].astype(F32).T.astype(BF16), tok[...]).astype(BF16)
+    sum_buf[...] = jnp.zeros_like(sum_buf)
+    for row, grad_map in ((0, grad_q_map), (1, grad_v_map)):
+        product_map = dot(grad_map, v_in[...]) * v_out_t[...].astype(F32)
+        out_row = out_scale[pl.ds(row, 1), pl.ds(half, 384)]
+        out_col = jnp.broadcast_to(out_row, (128, 384)).T[:, 0:1]
+        sum_buf[row : row + 1, :] = jnp.sum(product_map * out_col, axis=0, keepdims=True)
+        out_part = jnp.sum(product_map * rank_scale[pl.ds(row, 1), :], axis=1, keepdims=True)
+        out_part_row = jnp.broadcast_to(out_part, (384, 128)).T[0:1, :]
+        sum_buf[2 + row : 3 + row, pl.ds(half, 384)] = out_part_row
+
+    stages = (to_sib, to_near, to_far, {"batch": bx}, {"batch": by})
+    for k, where in enumerate(stages):
+        swap = remote(16 + k, sum_buf.at[pl.ds(8 * k, 8)], sum_recv.at[pl.ds(8 * k, 8)], where)
+        swap.start()
+        swap.wait_recv()
+        sum_buf[8 * k + 8 : 8 * k + 16, :] = (
+            sum_buf[8 * k : 8 * k + 8, :] + sum_recv[8 * k : 8 * k + 8, :]
+        )
+        swap.wait_send()
+    rank_total[...] = sum_buf[40:42, :]
+    out_total[...] = sum_buf[42:44, 0:768]
+
+    send_lo.wait_recv()
+    send_ig.wait_recv()
+    keep_lo.wait()
+    keep_ig.wait()
+    for item in (
+        send_far,
+        send_near,
+        send_sib,
+        pass_far_sib,
+        pass_far_near,
+        pass_near_sib,
+        pass_last,
+        send_og,
+        swap_att,
+        swap_ga,
+        send_lo,
+        swap_ta,
+        send_tn_far,
+        send_tn_own,
+        swap_tb,
+        send_ig,
+    ):
+        item.wait_send()
+
+
+def fast_body(
+    tokens,
+    attn_in_weight,
+    out_weight,
+    ffn_in_weight,
+    ffn_out_weight,
+    vera_in,
+    vera_out,
+    rank_scale,
+    out_scale,
+    gains,
+    shifts,
+    ffn_bias,
+    splits,
+    out_grad,
+):
+    hbm = pl.BlockSpec(memory_space=pl.ANY)
+    vmem = pl.BlockSpec(memory_space=pltpu.VMEM)
+    smem = pl.BlockSpec(memory_space=pltpu.SMEM)
+    shape = tokens.shape
+    scratch = [
+        ((1024, 768), BF16),
+        ((256, 768), BF16),
+        ((768, 1152), BF16),
+        ((768, 768), BF16),
+        ((768, 3072), BF16),
+        ((3072, 768), BF16),
+        ((768, 1024), BF16),
+        ((1024, 384), BF16),
+        ((384, 1024), BF16),
+        ((3, 1024, 256), BF16),
+        ((6, 512, 256), BF16),
+        ((3, 1024, 128), BF16),
+        ((384, 1024), BF16),
+        ((384, 1024), BF16),
+        ((6, 1024, 512), BF16),
+        ((1024, 512), F32),
+        ((384, 512), F32),
+        ((6, 1, 512), F32),
+        ((256, 384), BF16),
+        ((256, 384), BF16),
+        ((256, 768), F32),
+        ((256, 768), F32),
+        ((256, 768), F32),
+        ((256, 3072), F32),
+        ((256, 768), BF16),
+        ((256, 768), F32),
+        ((256, 768), F32),
+        ((256, 768), BF16),
+        ((256, 384), BF16),
+        ((256, 384), BF16),
+        ((256, 384), BF16),
+        ((6, 128, 512), BF16),
+        ((6, 512, 128), BF16),
+        ((6, 1, 512), F32),
+        ((1024, 768), BF16),
+        ((384, 512), F32),
+        ((256, 768), BF16),
+        ((256, 768), BF16),
+        ((256, 768), F32),
+        ((256, 768), BF16),
+        ((256, 768), BF16),
+        ((256, 768), BF16),
+        ((256, 768), BF16),
+        ((256, 768), BF16),
+        ((48, 1024), F32),
+        ((40, 1024), F32),
+    ]
+    layer_out, in_grad, rank_total, out_total = pl.pallas_call(
+        functools.partial(layer_kernel, 4),
+        out_shape=(
+            jax.ShapeDtypeStruct(shape, BF16),
+            jax.ShapeDtypeStruct(shape, BF16),
+            jax.ShapeDtypeStruct(rank_scale.shape, F32),
+            jax.ShapeDtypeStruct(out_scale.shape, F32),
+        ),
+        in_specs=[hbm] * 8 + [vmem] * 5 + [smem],
+        out_specs=(hbm, hbm, vmem, vmem),
+        scratch_shapes=[pltpu.VMEM(dims, kind) for dims, kind in scratch]
+        + [
+            pltpu.SemaphoreType.DMA((21,)),
+            pltpu.SemaphoreType.DMA((21,)),
+            pltpu.SemaphoreType.DMA((12,)),
+        ],
+        compiler_params=pltpu.CompilerParams(
+            collective_id=0, has_side_effects=True, vmem_limit_bytes=60 * 2**20
+        ),
+        name="encoder_layer",
+    )(
+        tokens,
+        attn_in_weight,
+        out_weight,
+        ffn_in_weight,
+        ffn_out_weight,
+        vera_in,
+        vera_out,
+        out_grad,
+        rank_scale,
+        out_scale,
+        gains,
+        shifts,
+        ffn_bias.reshape(1, -1),
+        splits,
+    )
+    scale_norms = jnp.concatenate(
+        [
+            jnp.sqrt(jnp.sum(rank_total * rank_total, axis=1)),
+            jnp.sqrt(jnp.sum(out_total * out_total, axis=1)),
+        ]
+    )
+    return layer_out, in_grad, rank_total, out_total, scale_norms
+
+
 def solution(mesh):
+    chosen = fast_body if fits(mesh) else body
     in_specs = (
         P("batch", "seq", None),
         P(),
@@ -253,4 +843,4 @@
         P("batch", "seq", None),
     )
     out_specs = (P("batch", "seq", None), P("batch", "seq", None), P(), P(), P())
-    return jax.shard_map(body, mesh=mesh, in_specs=in_specs, out_specs=out_specs, check_vma=False)
+    return jax.shard_map(chosen, mesh=mesh, in_specs=in_specs, out_specs=out_specs, check_vma=False)

time: 411 us -> 91.8 us (0.22)
  the two profiles are of different devices: /device:TPU:12 before, /device:TPU:0 now
where the time goes in v1:
time: 91.8 us; the launch traced here: 91.3 us
  Pallas kernels  82.3 us (90%)
  local copies, waits for them, and re-layouts  6.13 us (7%)
  other arithmetic  2.23 us (2%)
    pallas_call x1, Pallas kernels, fast_body(): pl.pallas_call(functools.partial(layer_kernel, 4), out_shape=(jax.ShapeDt...  82.3 us
    unnamed x4, local copies, waits for them, and re-layouts  6.11 us

profile of v1, /device:TPU:0, one launch (start us, length us, event | category | flops | bytes accessed | tf_op | source)
XLA Modules:
  0.0 91.3 jit_solution(3847547211670141725)
XLA Ops:
  0.6 82.3 %encoder_layer.1 = (bf16[2,128,768]{2,1,0:T(8,128)(2,1)}, bf16[2,128,768]{2,1,0:T(8,128)(2,1)}, f32[2,1024]{1,0:T(2,128)}, f32[2,768]{1,0:T(2,128)}) custom-call(bf16[2,128,768]{2,1,0:T(8,128)(2,1)} %tokens.1, bf16[768,2304]{1,0:T(8,128)(2,1)} %attn_in.1, bf16[768,768]{1,0:T(8,128)(2,1)} %out_w.1, bf16[768,3072]{1,0:T(8,128)(2,1)} %ffn_in.1, ...), custom_call_target="tpu_custom_call" | custom-call | tf_op jit(solution)/shard_map/encoder_layer/pallas_call | solution.py:782
  83.0 0.8 multiply_reduce_fusion.1
  83.8 0.8 multiply_reduce_fusion
  84.6 0.6 pad_maximum_fusion
  85.2 1.8 %copy.23 = bf16[2,128,768]{2,1,0:T(8,128)(2,1)} copy(bf16[2,128,768]{2,1,0:T(8,128)(2,1)} %get-tuple-element.18) | data formatting | bytes 786432
  87.0 1.8 %copy.24 = bf16[2,128,768]{2,1,0:T(8,128)(2,1)} copy(bf16[2,128,768]{2,1,0:T(8,128)(2,1)} %get-tuple-element.19) | data formatting | bytes 786432
  88.8 1.3 %copy.25 = f32[2,1024]{1,0:T(2,128)} copy(f32[2,1024]{1,0:T(2,128)} %get-tuple-element.20) | data formatting | bytes 16384
  90.1 1.3 %copy.26 = f32[2,768]{1,0:T(2,128)} copy(f32[2,768]{1,0:T(2,128)} %get-tuple-element.21) | data formatting | bytes 12288
  (2 shorter events, 0.0 us)

commit v2 on v1

--- a/solution.py
+++ b/solution.py
@@ -257,11 +257,11 @@
     return lax.dot_general(left, right, (((1,), (1,)), ((), ())), preferred_element_type=F32)
 
 
-OWN, FAR, SIB, SIB_FAR, NEAR, NEAR_FAR, SIB_NEAR, SIB_NEAR_FAR = range(8)
+OWN, SIB, FAR, SIB_FAR, NEAR_FAR, SIB_NEAR_FAR, NEAR, SIB_NEAR = range(8)
+PIECES = 4
 
 
 def layer_kernel(
-    n_batch,
     tokens,
     attn_in,
     out_w,
@@ -278,8 +278,7 @@
     splits,
     layer_out,
     in_grad,
-    rank_total,
-    out_total,
+    sums,
     tok,
     og,
     w_all,
@@ -316,13 +315,12 @@
     delta,
     d_kv,
     dq_t,
-    ta_send,
-    ta_recv,
-    ta_mine,
+    part_send,
+    part_recv,
+    part_mine,
+    far_terms,
     tn_send,
     tn_recv,
-    tb_send,
-    tb_recv,
     ig_buf,
     sum_buf,
     sum_recv,
@@ -358,7 +356,10 @@
     def block(ref, k, n=1):
         return ref.at[pl.ds(128 * k, 128 * n)]
 
+    near_far = far + near - s
     to_sib, to_near, to_far = {"seq": sib}, {"seq": near}, {"seq": far}
+    to_near_far = {"seq": near_far}
+    to_bx, to_by, to_bxy = {"batch": bx}, {"batch": by}, {"batch": bx + by - b}
 
     loads = [
         local(0, tokens.at[group], block(tok, OWN)),
@@ -370,25 +371,34 @@
         local(6, out_w, w_out),
         local(7, ffn_in, w_one),
         local(8, ffn_out, w_two),
-        local(9, out_grad.at[group], block(og, OWN)),
+        local(9, out_grad.at[group], og.at[pl.ds(0, 128)]),
     ]
     for item in loads:
         item.start()
 
     barrier = pltpu.get_barrier_semaphore()
-    for where in (to_sib, to_near, to_far, {"batch": bx}, {"batch": by}):
+    for where in (to_sib, to_near, to_far, to_near_far, to_bx, to_by, to_bxy):
         pl.semaphore_signal(barrier, inc=1, device_id=where, device_id_type=MESH)
-    pl.semaphore_wait(barrier, 5)
-
-    send_far = remote(0, tokens.at[1 - group], block(tok, FAR), to_far)
-    send_near = remote(1, tokens.at[group], block(tok, NEAR), to_near)
-    send_sib = remote(2, tokens.at[group], block(tok, SIB), to_sib)
-    pass_far_sib = remote(3, block(tok, FAR), block(tok, SIB_FAR), to_sib)
-    pass_far_near = remote(4, block(tok, FAR), block(tok, NEAR_FAR), to_near)
-    pass_near_sib = remote(5, block(tok, NEAR), block(tok, SIB_NEAR), to_sib)
-    pass_last = remote(6, block(tok, NEAR_FAR), block(tok, SIB_NEAR_FAR), to_sib)
-    send_og = remote(7, out_grad.at[1 - group], block(og, FAR), to_far)
-    send_far.start()
+    pl.semaphore_wait(barrier, 7)
+
+    piece = 128 // PIECES
+    send_far, pass_far_near, pass_last = [], [], []
+    for k in range(PIECES):
+        part = pl.ds(128 * FAR + piece * k, piece)
+        near_part = pl.ds(128 * NEAR_FAR + piece * k, piece)
+        last_part = pl.ds(128 * SIB_NEAR_FAR + piece * k, piece)
+        send_far.append(
+            remote(k, tokens.at[1 - group, pl.ds(piece * k, piece)], tok.at[part], to_far)
+        )
+        pass_far_near.append(remote(PIECES + k, tok.at[part], tok.at[near_part], to_near))
+        pass_last.append(remote(2 * PIECES + k, tok.at[near_part], tok.at[last_part], to_sib))
+    send_near = remote(12, tokens.at[group], block(tok, NEAR), to_near)
+    send_sib = remote(13, tokens.at[group], block(tok, SIB), to_sib)
+    pass_far_sib = remote(14, block(tok, FAR), block(tok, SIB_FAR), to_sib)
+    pass_near_sib = remote(15, block(tok, NEAR), block(tok, SIB_NEAR), to_sib)
+    send_og = remote(16, out_grad.at[1 - group], og.at[pl.ds(128, 128)], to_far)
+    for item in send_far:
+        item.start()
     send_near.start()
     send_sib.start()
 
@@ -412,16 +422,16 @@
     lane = lax.broadcasted_iota(jnp.int32, (128, 128), 1)
     row_at = lax.broadcasted_iota(jnp.int32, (128, 128), 0)
     flip_one, flip_two, flip_four = sib - s, near - s, far - s
-    starts = [
+    starts = (
         s,
+        s + flip_one,
         s + flip_four,
-        s + flip_one,
         s + flip_four + flip_one,
+        s + flip_two + flip_four,
+        s + flip_two + flip_four + flip_one,
         s + flip_two,
-        s + flip_two + flip_four,
         s + flip_two + flip_one,
-        s + flip_two + flip_four + flip_one,
-    ]
+    )
     for k in range(8):
         first = (starts[k] * 128 + row_at < split).astype(F32)
         second = 1.0 - first
@@ -439,51 +449,49 @@
     shift_v = shifts[1:2, pl.ds(half, 384)]
     low_lane = lax.broadcasted_iota(jnp.int32, (256, 128), 1) < 64
 
-    def project(one, two, queries):
-        rows = jnp.concatenate(
-            [tok[128 * one : 128 * one + 128, :], tok[128 * two : 128 * two + 128, :]], axis=0
-        )
+    def project(first, queries):
+        to = slice(128 * first, 128 * first + 256)
+        rows = tok[to, :]
         keys = dot(rows, w_all[:, 384:768])
         values = dot(rows, w_all[:, 768:1152]) + shift_v
         low_keys = keys.astype(BF16)
         low_values = values.astype(BF16)
-        keys_t = keys.T.astype(BF16)
-        values_t = values.T.astype(BF16)
-        for n, k in ((0, one), (1, two)):
-            part = slice(128 * n, 128 * n + 128)
-            to = slice(128 * k, 128 * k + 128)
-            for p in range(3):
-                k_ext[p, to, 0:128] = low_keys[part, 128 * p : 128 * p + 128]
-                val[p, to, :] = low_values[part, 128 * p : 128 * p + 128]
-            k_t[:, to] = keys_t[:, part]
-            v_t[:, to] = values_t[:, part]
+        for p in range(3):
+            k_ext[p, to, 0:128] = low_keys[:, 128 * p : 128 * p + 128]
+            val[p, to, :] = low_values[:, 128 * p : 128 * p + 128]
+        k_t[:, to] = keys.T.astype(BF16)
+        v_t[:, to] = values.T.astype(BF16)
         if queries:
             query = dot(rows, w_all[:, 0:384]) + shift_q
             low_query = query.astype(BF16).astype(F32) * 0.125
             for h in range(6):
                 p = h // 2
                 mine = low_lane if h % 2 == 0 else jnp.logical_not(low_lane)
-                masked = jnp.where(mine, low_query[:, 128 * p : 128 * p + 128], 0.0).astype(BF16)
-                for n, k in ((0, one), (1, two)):
-                    q_ext[h, 128 * k : 128 * k + 128, 0:128] = masked[128 * n : 128 * n + 128]
+                masked = jnp.where(mine, low_query[:, 128 * p : 128 * p + 128], 0.0)
+                q_ext[h, to, 0:128] = masked.astype(BF16)
 
     loads[0].wait()
     send_sib.wait_recv()
-    project(OWN, SIB, True)
-    send_near.wait_recv()
-    pass_near_sib.start()
-    send_far.wait_recv()
-    pass_far_near.start()
+    project(OWN, True)
+    for k in range(PIECES):
+        if k == PIECES - 1:
+            send_near.wait_recv()
+            pass_near_sib.start()
+            pass_near_sib.wait_recv()
+            project(NEAR, False)
+        send_far[k].wait_recv()
+        pass_far_near[k].start()
     pass_far_sib.start()
-    pass_near_sib.wait_recv()
-    project(NEAR, SIB_NEAR, False)
-    pass_far_sib.wait_recv()
-    project(FAR, SIB_FAR, True)
-    pass_far_near.wait_recv()
-    pass_last.start()
+    for k in range(PIECES):
+        pass_far_near[k].wait_recv()
+        pass_last[k].start()
+        if k == PIECES - 2:
+            pass_far_sib.wait_recv()
+            project(FAR, True)
     send_og.start()
-    pass_last.wait_recv()
-    project(NEAR_FAR, SIB_NEAR_FAR, False)
+    for k in range(PIECES):
+        pass_last[k].wait_recv()
+    project(NEAR_FAR, False)
 
     def forward_head(h, _):
         p = h // 2
@@ -509,8 +517,9 @@
 
     lax.fori_loop(0, 6, forward_head, 0)
 
-    swap_att = remote(8, att_send, att_recv, to_sib)
-    att_send[...] = att_t[:, 256:512].T.astype(BF16)
+    swap_att = remote(17, att_send, att_recv, to_sib)
+    for k, at in ((0, 128 * SIB), (128, 128 * SIB_FAR)):
+        att_send[k : k + 128, :] = att_t[:, at : at + 128].T.astype(BF16)
     swap_att.start()
 
     def norm(values_in):
@@ -527,10 +536,12 @@
         )
 
     loads[6].wait()
-    branch = dot(att_t[:, 0:256].T.astype(BF16), w_out[pl.ds(half, 384), :])
+    attended_mine = jnp.concatenate([att_t[:, 0:128], att_t[:, 256:384]], axis=1).T
+    token_rows = jnp.concatenate([tok[0:128, :], tok[256:384, :]], axis=0).astype(F32)
+    branch = dot(attended_mine.astype(BF16), w_out[pl.ds(half, 384), :])
     swap_att.wait_recv()
     branch = branch + dot(att_recv[...], w_out[pl.ds(other_half, 384), :]) + shifts[2:3, :]
-    normed_one, inverse_one = norm(tok[0:256, :].astype(F32) + branch)
+    normed_one, inverse_one = norm(token_rows + branch)
     n_one[...] = normed_one
     hidden = normed_one * gains[0:1, :] + shifts[4:5, :]
     hid[...] = hidden
@@ -552,8 +563,8 @@
     lax.fori_loop(0, 6, ffn_forward, 0)
     normed_two, inverse_two = norm(hid[...] + acc[...] + shifts[3:4, :])
     lo_buf[...] = (normed_two * gains[1:2, :] + shifts[5:6, :]).astype(BF16)
-    send_lo = remote(10, block(lo_buf, FAR), layer_out.at[group], to_far)
-    keep_lo = local(10, block(lo_buf, OWN), layer_out.at[group])
+    send_lo = remote(18, lo_buf.at[pl.ds(128, 128)], layer_out.at[group], to_far)
+    keep_lo = local(10, lo_buf.at[pl.ds(0, 128)], layer_out.at[group])
     send_lo.start()
     keep_lo.start()
     loads[9].wait()
@@ -574,13 +585,19 @@
     grad_one = norm_back(acc[...], n_one[...], inverse_one, gains[0:1, :])
     g_one[...] = grad_one
     low_one = grad_one.astype(BF16)
-    swap_ga = remote(9, ga_send, ga_recv, to_sib)
+    swap_ga = remote(19, ga_send, ga_recv, to_sib)
     ga_send[...] = dot_nt(low_one, w_out[pl.ds(other_half, 384), :]).astype(BF16)
     swap_ga.start()
     ga_mine[...] = dot_nt(low_one, w_out[pl.ds(half, 384), :]).astype(BF16)
     swap_ga.wait_recv()
 
-    go_full = jnp.concatenate([ga_mine[...], ga_recv[...]], axis=0).astype(F32).T
+    go_full = (
+        jnp.concatenate(
+            [ga_mine[0:128], ga_recv[0:128], ga_mine[128:256], ga_recv[128:256]], axis=0
+        )
+        .astype(F32)
+        .T
+    )
     top_rows = lax.broadcasted_iota(jnp.int32, (128, 512), 0) < 64
     for p in range(3):
         pair = go_full[128 * p : 128 * p + 128, :]
@@ -596,7 +613,7 @@
             delta[h] = jnp.sum(rounded * attended, axis=0, keepdims=True)
 
     def backward_pair(p, start, first):
-        rows = slice(start, start + 512)
+        rows = slice(start, start + 256)
         grad_keys = None
         grad_values = None
         for e in range(2):
@@ -617,54 +634,64 @@
         d_kv[rows, pl.ds(pl.multiple_of(p * 128, 128), 128)] = grad_keys.astype(BF16)
         d_kv[rows, pl.ds(pl.multiple_of(384 + p * 128, 128), 128)] = grad_values.astype(BF16)
 
-    def near_pair(p, _):
-        backward_pair(p, 512, True)
-        return 0
-
-    def own_pair(p, _):
-        backward_pair(p, 0, False)
-        return 0
-
-    lax.fori_loop(0, 3, near_pair, 0)
-    swap_ta = remote(11, ta_send, ta_recv, to_sib)
-    ta_send[...] = dot_nt(d_kv[768:1024, :], w_all[:, 384:1152]).astype(BF16)
-    swap_ta.start()
-    ta_mine[...] = dot_nt(d_kv[512:768, :], w_all[:, 384:1152])
-    lax.fori_loop(0, 1, own_pair, 0)
-    swap_ta.wait_recv()
-    tn_send[...] = (ta_mine[...] + ta_recv[...].astype(F32)).astype(BF16)
-    send_tn_far = remote(12, tn_send.at[pl.ds(128, 128)], tn_recv.at[pl.ds(128, 128)], to_near)
-    send_tn_own = remote(13, tn_send.at[pl.ds(0, 128)], tn_recv.at[pl.ds(0, 128)], to_near)
-    send_tn_far.start()
-    send_tn_own.start()
-    lax.fori_loop(1, 3, own_pair, 0)
+    def pairs(start, low, high):
+        def step(p, _):
+            backward_pair(p, start, start == 128 * NEAR_FAR)
+            return 0
+
+        lax.fori_loop(low, high, step, 0)
+
+    def token_terms(start):
+        return dot_nt(d_kv[start : start + 256, :], w_all[:, 384:1152])
+
+    swap_parts = [
+        remote(20 + k, part_send.at[pl.ds(128 * k, 128)], part_recv.at[pl.ds(128 * k, 128)], to_sib)
+        for k in range(4)
+    ]
+    send_parts = [
+        remote(24 + k, tn_send.at[pl.ds(128 * k, 128)], tn_recv.at[pl.ds(128 * k, 128)], to_near)
+        for k in range(2)
+    ]
+
+    def share(k, terms):
+        part_send[128 * k : 128 * k + 128, :] = terms[128:256].astype(BF16)
+        swap_parts[k].start()
+        part_mine[128 * k : 128 * k + 128, :] = terms[0:128]
+
+    def shared(k):
+        swap_parts[k].wait_recv()
+        rows = slice(128 * k, 128 * k + 128)
+        return part_mine[rows, :] + part_recv[rows, :].astype(F32)
+
+    def pass_on(k):
+        tn_send[128 * k : 128 * k + 128, :] = shared(k).astype(BF16)
+        send_parts[k].start()
+
+    pairs(128 * NEAR_FAR, 0, 3)
+    share(0, token_terms(128 * NEAR_FAR))
+    pairs(128 * NEAR, 0, 1)
+    pass_on(0)
+    pairs(128 * NEAR, 1, 3)
+    share(1, token_terms(128 * NEAR))
+    pairs(128 * FAR, 0, 1)
+    pass_on(1)
+    pairs(128 * FAR, 1, 3)
+    far_terms[...] = token_terms(128 * FAR)
+    pairs(128 * OWN, 0, 3)
+
+    low_dq = (dq_t[...] * 0.125).T.astype(BF16)
+    share(2, far_terms[...] + dot_nt(low_dq[256:512, :], w_all[:, 0:384]))
+    far_part = shared(2) + g_one[128:256, :]
+    send_parts[0].wait_recv()
+    ig_buf[128:256, :] = (far_part + tn_recv[0:128, :].astype(F32)).astype(BF16)
+    send_ig = remote(26, ig_buf.at[pl.ds(128, 128)], in_grad.at[group], to_far)
+    keep_ig = local(11, ig_buf.at[pl.ds(0, 128)], in_grad.at[group])
+    send_ig.start()
 
     low_dq_t = (dq_t[...] * 0.125).astype(BF16)
-    low_dq = (dq_t[...] * 0.125).T.astype(BF16)
-    swap_tb = remote(14, tb_send, tb_recv, to_sib)
-    tb_send[...] = (
-        dot_nt(d_kv[256:512, :], w_all[:, 384:1152]) + dot_nt(low_dq[256:512, :], w_all[:, 0:384])
-    ).astype(BF16)
-    swap_tb.start()
-    mine = (
-        g_one[...]
-        + dot_nt(d_kv[0:256, :], w_all[:, 384:1152])
-        + dot_nt(low_dq[0:256, :], w_all[:, 0:384])
-    )
-    swap_tb.wait_recv()
-    send_tn_far.wait_recv()
-    mine = mine + tb_recv[...].astype(F32)
-    ig_buf[128:256, :] = (mine[128:256] + tn_recv[128:256, :].astype(F32)).astype(BF16)
-    send_ig = remote(15, block(ig_buf, FAR), in_grad.at[group], to_far)
-    keep_ig = local(11, block(ig_buf, OWN), in_grad.at[group])
-    send_ig.start()
-    send_tn_own.wait_recv()
-    ig_buf[0:128, :] = (mine[0:128] + tn_recv[0:128, :].astype(F32)).astype(BF16)
-    keep_ig.start()
-
     grad_q_map = dot(low_dq_t, tok[0:512, :]).astype(BF16)
     grad_v_map = dot(d_kv[:, 384:768].astype(F32).T.astype(BF16), tok[...]).astype(BF16)
-    sum_buf[...] = jnp.zeros_like(sum_buf)
+    sum_buf[0:8, :] = jnp.zeros((8, 1024), F32)
     for row, grad_map in ((0, grad_q_map), (1, grad_v_map)):
         product_map = dot(grad_map, v_in[...]) * v_out_t[...].astype(F32)
         out_row = out_scale[pl.ds(row, 1), pl.ds(half, 384)]
@@ -674,41 +701,75 @@
         out_part_row = jnp.broadcast_to(out_part, (384, 128)).T[0:1, :]
         sum_buf[2 + row : 3 + row, pl.ds(half, 384)] = out_part_row
 
-    stages = (to_sib, to_near, to_far, {"batch": bx}, {"batch": by})
-    for k, where in enumerate(stages):
-        swap = remote(16 + k, sum_buf.at[pl.ds(8 * k, 8)], sum_recv.at[pl.ds(8 * k, 8)], where)
-        swap.start()
+    def exchange(k, stage, wheres):
+        swaps = [
+            remote(
+                k + n,
+                sum_buf.at[pl.ds(8 * stage, 8)],
+                sum_recv.at[pl.ds(8 * (k - 27 + n), 8)],
+                where,
+            )
+            for n, where in enumerate(wheres)
+        ]
+        for swap in swaps:
+            swap.start()
+        return swaps
+
+    def received(k):
+        return sum_recv[8 * k : 8 * k + 8, :]
+
+    core_swaps = exchange(27, 0, (to_sib,))
+    share(3, token_terms(128 * OWN) + dot_nt(low_dq[0:256, :], w_all[:, 0:384]))
+    core_swaps[0].wait_recv()
+    sum_buf[8:16, :] = sum_buf[0:8, :] + received(0)
+    plane_swaps = exchange(28, 1, (to_bx, to_by, to_bxy))
+    own_part = shared(3) + g_one[0:128, :]
+    send_parts[1].wait_recv()
+    ig_buf[0:128, :] = (own_part + tn_recv[128:256, :].astype(F32)).astype(BF16)
+    keep_ig.start()
+    for swap in plane_swaps:
         swap.wait_recv()
-        sum_buf[8 * k + 8 : 8 * k + 16, :] = (
-            sum_buf[8 * k : 8 * k + 8, :] + sum_recv[8 * k : 8 * k + 8, :]
-        )
-        swap.wait_send()
-    rank_total[...] = sum_buf[40:42, :]
-    out_total[...] = sum_buf[42:44, 0:768]
+    sum_buf[16:24, :] = (sum_buf[8:16, :] + received(1)) + (received(2) + received(3))
+    line_swaps = exchange(31, 2, (to_near, to_far, to_near_far))
+    for swap in line_swaps:
+        swap.wait_recv()
+    sums[...] = (sum_buf[16:24, :] + received(4)) + (received(5) + received(6))
 
     send_lo.wait_recv()
     send_ig.wait_recv()
     keep_lo.wait()
     keep_ig.wait()
     for item in (
-        send_far,
+        *send_far,
+        *pass_far_near,
+        *pass_last,
         send_near,
         send_sib,
         pass_far_sib,
-        pass_far_near,
         pass_near_sib,
-        pass_last,
         send_og,
         swap_att,
         swap_ga,
         send_lo,
-        swap_ta,
-        send_tn_far,
-        send_tn_own,
-        swap_tb,
+        *swap_parts,
+        *send_parts,
         send_ig,
+        *core_swaps,
+        *plane_swaps,
+        *line_swaps,
     ):
         item.wait_send()
+
+
+def finish_kernel(layer_in, grad_in, sums, layer_out, in_grad, rank_total, out_total, norms):
+    layer_out[...] = layer_in[...]
+    in_grad[...] = grad_in[...]
+    rank_total[...] = sums[0:2, :]
+    out_total[...] = sums[2:4, 0:768]
+    totals = sums[0:4, :]
+    lengths = jnp.sqrt(jnp.sum(totals * totals, axis=1, keepdims=True))
+    for k in range(4):
+        norms[k] = lengths[k, 0]
 
 
 def fast_body(
@@ -768,31 +829,26 @@
         ((6, 1, 512), F32),
         ((1024, 768), BF16),
         ((384, 512), F32),
-        ((256, 768), BF16),
-        ((256, 768), BF16),
+        ((512, 768), BF16),
+        ((512, 768), BF16),
+        ((512, 768), F32),
         ((256, 768), F32),
         ((256, 768), BF16),
         ((256, 768), BF16),
         ((256, 768), BF16),
-        ((256, 768), BF16),
-        ((256, 768), BF16),
-        ((48, 1024), F32),
-        ((40, 1024), F32),
+        ((24, 1024), F32),
+        ((56, 1024), F32),
     ]
-    layer_out, in_grad, rank_total, out_total = pl.pallas_call(
-        functools.partial(layer_kernel, 4),
-        out_shape=(
-            jax.ShapeDtypeStruct(shape, BF16),
-            jax.ShapeDtypeStruct(shape, BF16),
-            jax.ShapeDtypeStruct(rank_scale.shape, F32),
-            jax.ShapeDtypeStruct(out_scale.shape, F32),
-        ),
+    rows_type = jax.ShapeDtypeStruct(shape, BF16)
+    layer_rows, grad_rows, sums = pl.pallas_call(
+        layer_kernel,
+        out_shape=(rows_type, rows_type, jax.ShapeDtypeStruct((8, 1024), F32)),
         in_specs=[hbm] * 8 + [vmem] * 5 + [smem],
-        out_specs=(hbm, hbm, vmem, vmem),
+        out_specs=(hbm, hbm, vmem),
         scratch_shapes=[pltpu.VMEM(dims, kind) for dims, kind in scratch]
         + [
-            pltpu.SemaphoreType.DMA((21,)),
-            pltpu.SemaphoreType.DMA((21,)),
+            pltpu.SemaphoreType.DMA((34,)),
+            pltpu.SemaphoreType.DMA((34,)),
             pltpu.SemaphoreType.DMA((12,)),
         ],
         compiler_params=pltpu.CompilerParams(
@@ -815,13 +871,19 @@
         ffn_bias.reshape(1, -1),
         splits,
     )
-    scale_norms = jnp.concatenate(
-        [
-            jnp.sqrt(jnp.sum(rank_total * rank_total, axis=1)),
-            jnp.sqrt(jnp.sum(out_total * out_total, axis=1)),
-        ]
-    )
-    return layer_out, in_grad, rank_total, out_total, scale_norms
+    return pl.pallas_call(
+        finish_kernel,
+        out_shape=(
+            rows_type,
+            rows_type,
+            jax.ShapeDtypeStruct(rank_scale.shape, F32),
+            jax.ShapeDtypeStruct(out_scale.shape, F32),
+            jax.ShapeDtypeStruct((4,), F32),
+        ),
+        in_specs=[vmem, vmem, vmem],
+        out_specs=(vmem, vmem, vmem, vmem, smem),
+        name="finish",
+    )(layer_rows, grad_rows, sums)
 
 
 def solution(mesh):

time: 91.8 us -> 75.4 us (0.82)
  Pallas kernels: 82.3 us -> 74.4 us
  local copies, waits for them, and re-layouts: 6.13 us -> 0 us
  other arithmetic: 2.23 us -> 0 us
    pallas_call x1 -> x2, Pallas kernels: 82.3 us -> 74.4 us  [the longest x1 72.4 us: fast_body(): pl.pallas_call(layer_kernel, out_shape=(rows_type, rows_type, jax.ShapeDt...]
    unnamed x4 -> x0, local copies, waits for them, and re-layouts: 6.11 us -> none
    reduce_sum x2 -> x0, other arithmetic: 1.64 us -> none  [the longest x1 0.82 us: fast_body(): jnp.sum(rank_total * rank_total, axis=1)]
where the time goes in v2:
time: 75.4 us; the launch traced here: 75.2 us
  Pallas kernels  74.4 us (99%)
  between operations  0.81 us (1%)
    pallas_call x1, Pallas kernels, fast_body(): pl.pallas_call(layer_kernel, out_shape=(rows_type, rows_type, jax.ShapeDt...  72.4 us
    pallas_call x1, Pallas kernels, fast_body(): pl.pallas_call(finish_kernel, out_shape=(rows_type, rows_type, jax.ShapeD...  2.04 us

profile of v2, /device:TPU:0, one launch (start us, length us, event | category | flops | bytes accessed | tf_op | source)
XLA Modules:
  0.0 75.2 jit_solution(13028794876058747211)
XLA Ops:
  0.6 72.4 %encoder_layer.1 = (bf16[2,128,768]{2,1,0:T(8,128)(2,1)}, bf16[2,128,768]{2,1,0:T(8,128)(2,1)}, f32[8,1024]{1,0:T(8,128)}) custom-call(bf16[2,128,768]{2,1,0:T(8,128)(2,1)} %tokens.1, bf16[768,2304]{1,0:T(8,128)(2,1)} %attn_in.1, bf16[768,768]{1,0:T(8,128)(2,1)} %out_w.1, bf16[768,3072]{1,0:T(8,128)(2,1)} %ffn_in.1, bf16[3072,768]{1,0:T(8,128)(2,1)} %ffn_out.1, ...), custom_call_target="tpu_custom_call" | custom-call | tf_op jit(solution)/shard_map/encoder_layer/pallas_call | solution.py:843
  73.0 2.0 %finish.1 = (bf16[2,128,768]{2,1,0:T(8,128)(2,1)}, bf16[2,128,768]{2,1,0:T(8,128)(2,1)}, f32[2,1024]{1,0:T(2,128)}, f32[2,768]{1,0:T(2,128)}, f32[4]{0:T(128)}) custom-call(bf16[2,128,768]{2,1,0:T(8,128)(2,1)} %get-tuple-element.8.layer_in, bf16[2,128,768]{2,1,0:T(8,128)(2,1)} %get-tuple-element.9.grad_in, f32[8,1024]{1,0:T(8,128)} %get-tuple-element.10.sums), custom_call_target="tpu_custom_call" | custom-call | tf_op jit(solution)/shard_map/finish/pallas_call | solution.py:874

commit v3 on v2

--- a/solution.py
+++ b/solution.py
@@ -259,6 +259,7 @@
 
 OWN, SIB, FAR, SIB_FAR, NEAR_FAR, SIB_NEAR_FAR, NEAR, SIB_NEAR = range(8)
 PIECES = 4
+PART_OWN, PART_FAR, PART_LAST = range(3)
 
 
 def layer_kernel(
@@ -296,12 +297,15 @@
     probs,
     s_buf,
     att_t,
-    inv_l,
+    part_top,
+    part_sum,
+    part_out,
+    share,
     att_send,
     att_recv,
     hid,
     n_one,
-    acc,
+    wide,
     gprime,
     low_rows,
     g_two,
@@ -470,52 +474,82 @@
                 masked = jnp.where(mine, low_query[:, 128 * p : 128 * p + 128], 0.0)
                 q_ext[h, to, 0:128] = masked.astype(BF16)
 
+    def attend(group_at, starts_at, first_query, count):
+        queries = slice(first_query, first_query + count)
+        peaks, totals, outs = {}, {}, {}
+
+        def scores(h, at):
+            part = dot_nt(k_ext[h // 2, at : at + 256, :], q_ext[h, queries, :])
+            s_buf[h % 2, at : at + 256, queries] = part
+            peak = jnp.max(part, axis=0, keepdims=True)
+            peaks[h] = jnp.maximum(peaks[h], peak) if h in peaks else peak
+
+        def weights(h, at):
+            weight = jnp.exp(s_buf[h % 2, at : at + 256, queries] - peaks[h])
+            total = jnp.sum(weight, axis=0, keepdims=True)
+            low_weight = weight.astype(BF16)
+            probs[h, at : at + 256, queries] = low_weight
+            out = dot(v_t[64 * h : 64 * h + 64, at : at + 256], low_weight)
+            totals[h] = totals[h] + total if h in totals else total
+            outs[h] = outs[h] + out if h in outs else out
+
+        for at in starts_at:
+            scores(0, at)
+        for h in range(6):
+            for at in starts_at:
+                if h < 5:
+                    scores(h + 1, at)
+                weights(h, at)
+            part_top[group_at, h, :, queries] = peaks[h]
+            part_sum[group_at, h, :, queries] = totals[h]
+            part_out[group_at, 64 * h : 64 * h + 64, queries] = outs[h]
+
+    def combine(first_query, groups):
+        queries = slice(first_query, first_query + 256)
+        for h in range(6):
+            rows_h = slice(64 * h, 64 * h + 64)
+            tops = [part_top[g, h, :, queries] for g in groups]
+            top = functools.reduce(jnp.maximum, tops)
+            shares = [jnp.exp(one - top) for one in tops]
+            total = functools.reduce(
+                jnp.add, [w * part_sum[g, h, :, queries] for w, g in zip(shares, groups)]
+            )
+            inverse = 1.0 / total
+            shares = [w * inverse for w in shares]
+            att_t[rows_h, queries] = functools.reduce(
+                jnp.add, [w * part_out[g, rows_h, queries] for w, g in zip(shares, groups)]
+            )
+            for w, g in zip(shares, groups):
+                share[g, h, :, queries] = w
+            if len(groups) == 2:
+                share[PART_FAR, h, :, queries] = shares[0]
+
     loads[0].wait()
     send_sib.wait_recv()
     project(OWN, True)
+    send_near.wait_recv()
+    pass_near_sib.start()
+    pass_near_sib.wait_recv()
+    project(NEAR, False)
+    attend(PART_OWN, (128 * OWN, 128 * NEAR), 0, 256)
     for k in range(PIECES):
-        if k == PIECES - 1:
-            send_near.wait_recv()
-            pass_near_sib.start()
-            pass_near_sib.wait_recv()
-            project(NEAR, False)
         send_far[k].wait_recv()
         pass_far_near[k].start()
     pass_far_sib.start()
+    pass_far_sib.wait_recv()
+    project(FAR, True)
+    attend(PART_FAR, (128 * FAR,), 0, 256)
+    attend(PART_OWN, (128 * OWN, 128 * NEAR, 128 * FAR), 256, 256)
     for k in range(PIECES):
         pass_far_near[k].wait_recv()
         pass_last[k].start()
-        if k == PIECES - 2:
-            pass_far_sib.wait_recv()
-            project(FAR, True)
     send_og.start()
     for k in range(PIECES):
         pass_last[k].wait_recv()
     project(NEAR_FAR, False)
-
-    def forward_head(h, _):
-        p = h // 2
-        rows_h = pl.ds(pl.multiple_of(h * 64, 64), 64)
-        top = None
-        for k in range(4):
-            part = dot_nt(k_ext[p, 256 * k : 256 * k + 256, :], q_ext[h])
-            s_buf[256 * k : 256 * k + 256, :] = part
-            peak = jnp.max(part, axis=0, keepdims=True)
-            top = peak if top is None else jnp.maximum(top, peak)
-        total = jnp.zeros((1, 512), F32)
-        out = jnp.zeros((64, 512), F32)
-        for k in range(4):
-            weight = jnp.exp(s_buf[256 * k : 256 * k + 256, :] - top)
-            total = total + jnp.sum(weight, axis=0, keepdims=True)
-            low_weight = weight.astype(BF16)
-            probs[h, 256 * k : 256 * k + 256, :] = low_weight
-            out = out + dot(v_t[rows_h, 256 * k : 256 * k + 256], low_weight)
-        inverse = 1.0 / total
-        inv_l[h] = inverse
-        att_t[rows_h, :] = out * inverse
-        return 0
-
-    lax.fori_loop(0, 6, forward_head, 0)
+    attend(PART_LAST, (128 * NEAR_FAR,), 0, 512)
+    combine(0, (PART_OWN, PART_FAR, PART_LAST))
+    combine(256, (PART_OWN, PART_LAST))
 
     swap_att = remote(17, att_send, att_recv, to_sib)
     for k, at in ((0, 128 * SIB), (128, 128 * SIB_FAR)):
@@ -549,19 +583,15 @@
 
     loads[7].wait()
     loads[8].wait()
-    acc[...] = jnp.zeros_like(acc)
-
-    def ffn_forward(t, _):
-        cols = pl.ds(pl.multiple_of(t * 512, 512), 512)
+    for t in range(0, 3072, 512):
+        cols = slice(t, t + 512)
         inner = dot(low_rows[...], w_one[:, cols]) + ffn_bias[:, cols]
         phi = 0.5 * (1.0 + lax.erf(inner * 0.7071067811865476))
         density = 0.3989422804014327 * jnp.exp(-0.5 * inner * inner)
         gprime[:, cols] = phi + inner * density
-        acc[...] += dot((inner * phi).astype(BF16), w_two[cols, :])
-        return 0
-
-    lax.fori_loop(0, 6, ffn_forward, 0)
-    normed_two, inverse_two = norm(hid[...] + acc[...] + shifts[3:4, :])
+        wide[:, cols] = (inner * phi).astype(BF16)
+    ffn_branch = dot(wide[...], w_two[...])
+    normed_two, inverse_two = norm(hid[...] + ffn_branch + shifts[3:4, :])
     lo_buf[...] = (normed_two * gains[1:2, :] + shifts[5:6, :]).astype(BF16)
     send_lo = remote(18, lo_buf.at[pl.ds(128, 128)], layer_out.at[group], to_far)
     keep_lo = local(10, lo_buf.at[pl.ds(0, 128)], layer_out.at[group])
@@ -572,74 +602,69 @@
     grad_two = norm_back(og[...].astype(F32), normed_two, inverse_two, gains[1:2, :])
     g_two[...] = grad_two
     low_rows[...] = grad_two.astype(BF16)
-    acc[...] = grad_two
-
-    def ffn_backward(t, _):
-        cols = pl.ds(pl.multiple_of(t * 512, 512), 512)
+    for t in range(0, 3072, 512):
+        cols = slice(t, t + 512)
         grad_act = dot_nt(low_rows[...], w_two[cols, :])
-        grad_inner = (grad_act * gprime[:, cols]).astype(BF16)
-        acc[...] += dot_nt(grad_inner, w_one[:, cols])
-        return 0
-
-    lax.fori_loop(0, 6, ffn_backward, 0)
-    grad_one = norm_back(acc[...], n_one[...], inverse_one, gains[0:1, :])
+        wide[:, cols] = (grad_act * gprime[:, cols]).astype(BF16)
+    grad_hidden = g_two[...] + dot_nt(wide[...], w_one[...])
+    grad_one = norm_back(grad_hidden, n_one[...], inverse_one, gains[0:1, :])
     g_one[...] = grad_one
     low_one = grad_one.astype(BF16)
     swap_ga = remote(19, ga_send, ga_recv, to_sib)
     ga_send[...] = dot_nt(low_one, w_out[pl.ds(other_half, 384), :]).astype(BF16)
     swap_ga.start()
     ga_mine[...] = dot_nt(low_one, w_out[pl.ds(half, 384), :]).astype(BF16)
+
+    low_row = lax.broadcasted_iota(jnp.int32, (128, 128), 0) < 64
+    low_col = lax.broadcasted_iota(jnp.int32, (128, 128), 1) < 64
+
+    def spread(block_at, rows):
+        to = slice(128 * block_at, 128 * block_at + 128)
+        flipped = rows.T
+        for p in range(3):
+            cols = slice(128 * p, 128 * p + 128)
+            for e in range(2):
+                h = 2 * p + e
+                rows_of = low_row if e == 0 else jnp.logical_not(low_row)
+                cols_of = low_col if e == 0 else jnp.logical_not(low_col)
+                go_m[h, to, :] = jnp.where(cols_of, rows[:, cols], 0.0).astype(BF16)
+                mine = jnp.where(rows_of, flipped[cols, :], 0.0)
+                go_t[h, :, to] = mine.astype(BF16)
+                delta[h, :, to] = jnp.sum(mine * att_t[cols, to], axis=0, keepdims=True)
+
+    spread(OWN, ga_mine[0:128, :].astype(F32))
+    spread(FAR, ga_mine[128:256, :].astype(F32))
     swap_ga.wait_recv()
-
-    go_full = (
-        jnp.concatenate(
-            [ga_mine[0:128], ga_recv[0:128], ga_mine[128:256], ga_recv[128:256]], axis=0
-        )
-        .astype(F32)
-        .T
-    )
-    top_rows = lax.broadcasted_iota(jnp.int32, (128, 512), 0) < 64
-    for p in range(3):
-        pair = go_full[128 * p : 128 * p + 128, :]
-        attended = att_t[128 * p : 128 * p + 128, :]
-        for e in range(2):
-            h = 2 * p + e
-            mine = top_rows if e == 0 else jnp.logical_not(top_rows)
-            scaled = jnp.where(mine, pair * inv_l[h], 0.0)
-            low_scaled = scaled.astype(BF16)
-            rounded = low_scaled.astype(F32)
-            go_t[h] = low_scaled
-            go_m[h] = rounded.T.astype(BF16)
-            delta[h] = jnp.sum(rounded * attended, axis=0, keepdims=True)
-
-    def backward_pair(p, start, first):
-        rows = slice(start, start + 256)
-        grad_keys = None
-        grad_values = None
-        for e in range(2):
-            h = 2 * p + e
-            rows_h = pl.ds(pl.multiple_of(h * 64, 64), 64)
-            weight = probs[h, rows, :]
-            grad_prob = dot(val[p, rows, :], go_t[h])
-            grad_score = (weight.astype(F32) * (grad_prob - delta[h])).astype(BF16)
-            value_part = dot(weight, go_m[h])
+    spread(SIB, ga_recv[0:128, :].astype(F32))
+    spread(SIB_FAR, ga_recv[128:256, :].astype(F32))
+
+    def backward(first, group_at, from_head, to_head):
+        rows = slice(128 * first, 128 * first + 256)
+
+        def value_dots(h):
+            return dot(val[h // 2, rows, :], go_t[h])
+
+        grad_prob = value_dots(from_head)
+        for h in range(from_head, to_head):
+            following = value_dots(h + 1) if h + 1 < to_head else None
+            weight = probs[h, rows, :].astype(F32) * share[group_at, h]
+            grad_score = (weight * (grad_prob - delta[h])).astype(BF16)
+            value_part = dot(weight.astype(BF16), go_m[h])
             key_part = dot(grad_score, q_ext[h, :, 0:128])
+            rows_h = slice(64 * h, 64 * h + 64)
             query_part = dot(k_t[rows_h, rows], grad_score)
-            grad_values = value_part if e == 0 else grad_values + value_part
-            grad_keys = key_part if e == 0 else grad_keys + key_part
-            if first:
+            if first == NEAR_FAR:
                 dq_t[rows_h, :] = query_part
             else:
                 dq_t[rows_h, :] += query_part
-        d_kv[rows, pl.ds(pl.multiple_of(p * 128, 128), 128)] = grad_keys.astype(BF16)
-        d_kv[rows, pl.ds(pl.multiple_of(384 + p * 128, 128), 128)] = grad_values.astype(BF16)
-
-    def pairs(start, low, high):
-        def step(p, _):
-            backward_pair(p, start, start == 128 * NEAR_FAR)
-            return 0
-
-        lax.fori_loop(low, high, step, 0)
+            if h % 2 == 0:
+                grad_values, grad_keys = value_part, key_part
+            else:
+                cols = slice(64 * h - 64, 64 * h + 64)
+                value_cols = slice(64 * h + 320, 64 * h + 448)
+                d_kv[rows, cols] = (grad_keys + key_part).astype(BF16)
+                d_kv[rows, value_cols] = (grad_values + value_part).astype(BF16)
+            grad_prob = following
 
     def token_terms(start):
         return dot_nt(d_kv[start : start + 256, :], w_all[:, 384:1152])
@@ -653,7 +678,7 @@
         for k in range(2)
     ]
 
-    def share(k, terms):
+    def share_out(k, terms):
         part_send[128 * k : 128 * k + 128, :] = terms[128:256].astype(BF16)
         swap_parts[k].start()
         part_mine[128 * k : 128 * k + 128, :] = terms[0:128]
@@ -667,20 +692,20 @@
         tn_send[128 * k : 128 * k + 128, :] = shared(k).astype(BF16)
         send_parts[k].start()
 
-    pairs(128 * NEAR_FAR, 0, 3)
-    share(0, token_terms(128 * NEAR_FAR))
-    pairs(128 * NEAR, 0, 1)
+    backward(NEAR_FAR, PART_LAST, 0, 6)
+    share_out(0, token_terms(128 * NEAR_FAR))
+    backward(NEAR, PART_OWN, 0, 2)
     pass_on(0)
-    pairs(128 * NEAR, 1, 3)
-    share(1, token_terms(128 * NEAR))
-    pairs(128 * FAR, 0, 1)
+    backward(NEAR, PART_OWN, 2, 6)
+    share_out(1, token_terms(128 * NEAR))
+    backward(FAR, PART_FAR, 0, 2)
     pass_on(1)
-    pairs(128 * FAR, 1, 3)
+    backward(FAR, PART_FAR, 2, 6)
     far_terms[...] = token_terms(128 * FAR)
-    pairs(128 * OWN, 0, 3)
+    backward(OWN, PART_OWN, 0, 6)
 
     low_dq = (dq_t[...] * 0.125).T.astype(BF16)
-    share(2, far_terms[...] + dot_nt(low_dq[256:512, :], w_all[:, 0:384]))
+    share_out(2, far_terms[...] + dot_nt(low_dq[256:512, :], w_all[:, 0:384]))
     far_part = shared(2) + g_one[128:256, :]
     send_parts[0].wait_recv()
     ig_buf[128:256, :] = (far_part + tn_recv[0:128, :].astype(F32)).astype(BF16)
@@ -719,7 +744,7 @@
         return sum_recv[8 * k : 8 * k + 8, :]
 
     core_swaps = exchange(27, 0, (to_sib,))
-    share(3, token_terms(128 * OWN) + dot_nt(low_dq[0:256, :], w_all[:, 0:384]))
+    share_out(3, token_terms(128 * OWN) + dot_nt(low_dq[0:256, :], w_all[:, 0:384]))
     core_swaps[0].wait_recv()
     sum_buf[8:16, :] = sum_buf[0:8, :] + received(0)
     plane_swaps = exchange(28, 1, (to_bx, to_by, to_bxy))
@@ -808,14 +833,17 @@
         ((384, 1024), BF16),
         ((384, 1024), BF16),
         ((6, 1024, 512), BF16),
-        ((1024, 512), F32),
+        ((2, 1024, 512), F32),
         ((384, 512), F32),
-        ((6, 1, 512), F32),
+        ((3, 6, 1, 512), F32),
+        ((3, 6, 1, 512), F32),
+        ((3, 384, 512), F32),
+        ((3, 6, 1, 512), F32),
         ((256, 384), BF16),
         ((256, 384), BF16),
         ((256, 768), F32),
         ((256, 768), F32),
-        ((256, 768), F32),
+        ((256, 3072), BF16),
         ((256, 3072), F32),
         ((256, 768), BF16),
         ((256, 768), F32),

time: 75.4 us -> 67.3 us (0.89)
  Pallas kernels: 74.4 us -> 66.3 us
    pallas_call x1, Pallas kernels: 72.4 us -> 64.2 us  [fast_body(): pl.pallas_call(layer_kernel, out_shape=(rows_type, rows_type, jax.ShapeDt...]
where the time goes in v3:
time: 67.3 us; the launch traced here: 67.1 us
  Pallas kernels  66.3 us (99%)
  between operations  0.81 us (1%)
    pallas_call x1, Pallas kernels, fast_body(): pl.pallas_call(layer_kernel, out_shape=(rows_type, rows_type, jax.ShapeDt...  64.2 us
    pallas_call x1, Pallas kernels, fast_body(): pl.pallas_call(finish_kernel, out_shape=(rows_type, rows_type, jax.ShapeD...  2.04 us

profile of v3, /device:TPU:0, one launch (start us, length us, event | category | flops | bytes accessed | tf_op | source)
XLA Modules:
  0.0 67.1 jit_solution(3113074092837001716)
XLA Ops:
  0.6 64.2 %encoder_layer.1 = (bf16[2,128,768]{2,1,0:T(8,128)(2,1)}, bf16[2,128,768]{2,1,0:T(8,128)(2,1)}, f32[8,1024]{1,0:T(8,128)}) custom-call(bf16[2,128,768]{2,1,0:T(8,128)(2,1)} %tokens.1, bf16[768,2304]{1,0:T(8,128)(2,1)} %attn_in.1, bf16[768,768]{1,0:T(8,128)(2,1)} %out_w.1, bf16[768,3072]{1,0:T(8,128)(2,1)} %ffn_in.1, bf16[3072,768]{1,0:T(8,128)(2,1)} %ffn_out.1, ...), custom_call_target="tpu_custom_call" | custom-call | tf_op jit(solution)/shard_map/encoder_layer/pallas_call | solution.py:871
  64.9 2.0 %finish.1 = (bf16[2,128,768]{2,1,0:T(8,128)(2,1)}, bf16[2,128,768]{2,1,0:T(8,128)(2,1)}, f32[2,1024]{1,0:T(2,128)}, f32[2,768]{1,0:T(2,128)}, f32[4]{0:T(128)}) custom-call(bf16[2,128,768]{2,1,0:T(8,128)(2,1)} %get-tuple-element.8.layer_in, bf16[2,128,768]{2,1,0:T(8,128)(2,1)} %get-tuple-element.9.grad_in, f32[8,1024]{1,0:T(8,128)} %get-tuple-element.10.sums), custom_call_target="tpu_custom_call" | custom-call | tf_op jit(solution)/shard_map/finish/pallas_call | solution.py:902

commit v4 on v3

--- a/solution.py
+++ b/solution.py
@@ -258,7 +258,7 @@
 
 
 OWN, SIB, FAR, SIB_FAR, NEAR_FAR, SIB_NEAR_FAR, NEAR, SIB_NEAR = range(8)
-PIECES = 4
+PIECES = 2
 PART_OWN, PART_FAR, PART_LAST = range(3)
 
 
@@ -271,15 +271,21 @@
     vera_in,
     vera_out,
     out_grad,
+    rank_scale_in,
+    out_scale_in,
+    gains_in,
+    shifts_in,
+    ffn_bias_in,
+    splits_in,
+    layer_out,
+    in_grad,
+    sums,
     rank_scale,
     out_scale,
     gains,
     shifts,
     ffn_bias,
     splits,
-    layer_out,
-    in_grad,
-    sums,
     tok,
     og,
     w_all,
@@ -289,6 +295,7 @@
     v_in,
     v_out,
     v_out_t,
+    rank_in,
     k_ext,
     q_ext,
     val,
@@ -318,6 +325,7 @@
     go_m,
     delta,
     d_kv,
+    d_held,
     dq_t,
     part_send,
     part_recv,
@@ -365,6 +373,10 @@
     to_near_far = {"seq": near_far}
     to_bx, to_by, to_bxy = {"batch": bx}, {"batch": by}, {"batch": bx + by - b}
 
+    barrier = pltpu.get_barrier_semaphore()
+    for where in (to_sib, to_near, to_far, to_near_far, to_bx, to_by, to_bxy):
+        pl.semaphore_signal(barrier, inc=1, device_id=where, device_id_type=MESH)
+
     loads = [
         local(0, tokens.at[group], block(tok, OWN)),
         local(1, vera_in, v_in),
@@ -377,12 +389,16 @@
         local(8, ffn_out, w_two),
         local(9, out_grad.at[group], og.at[pl.ds(0, 128)]),
     ]
-    for item in loads:
+    small_loads = [
+        local(12, rank_scale_in, rank_scale),
+        local(13, out_scale_in, out_scale),
+        local(14, gains_in, gains),
+        local(15, shifts_in, shifts),
+        local(16, ffn_bias_in, ffn_bias),
+        local(17, splits_in, splits),
+    ]
+    for item in (*small_loads, *loads):
         item.start()
-
-    barrier = pltpu.get_barrier_semaphore()
-    for where in (to_sib, to_near, to_far, to_near_far, to_bx, to_by, to_bxy):
-        pl.semaphore_signal(barrier, inc=1, device_id=where, device_id_type=MESH)
     pl.semaphore_wait(barrier, 7)
 
     piece = 128 // PIECES
@@ -401,13 +417,13 @@
     pass_far_sib = remote(14, block(tok, FAR), block(tok, SIB_FAR), to_sib)
     pass_near_sib = remote(15, block(tok, NEAR), block(tok, SIB_NEAR), to_sib)
     send_og = remote(16, out_grad.at[1 - group], og.at[pl.ds(128, 128)], to_far)
+    send_near.start()
+    send_sib.start()
     for item in send_far:
         item.start()
-    send_near.start()
-    send_sib.start()
-
-    for k in range(1, 6):
-        loads[k].wait()
+
+    for item in (*small_loads, *loads[1:6]):
+        item.wait()
     for row, at in ((0, 0), (1, 768)):
         scale_row = rank_scale[pl.ds(row, 1), :]
         out_row = out_scale[pl.ds(row, 1), pl.ds(half, 384)]
@@ -524,18 +540,24 @@
             if len(groups) == 2:
                 share[PART_FAR, h, :, queries] = shares[0]
 
+    def rank_rows(first):
+        to = slice(128 * first, 128 * first + 256)
+        rank_in[to, :] = dot(tok[to, :], v_in[...]).astype(BF16)
+
     loads[0].wait()
     send_sib.wait_recv()
     project(OWN, True)
+    rank_rows(OWN)
     send_near.wait_recv()
     pass_near_sib.start()
     pass_near_sib.wait_recv()
     project(NEAR, False)
-    attend(PART_OWN, (128 * OWN, 128 * NEAR), 0, 256)
+    rank_rows(NEAR)
     for k in range(PIECES):
         send_far[k].wait_recv()
         pass_far_near[k].start()
     pass_far_sib.start()
+    attend(PART_OWN, (128 * OWN, 128 * NEAR), 0, 256)
     pass_far_sib.wait_recv()
     project(FAR, True)
     attend(PART_FAR, (128 * FAR,), 0, 256)
@@ -544,6 +566,7 @@
         pass_far_near[k].wait_recv()
         pass_last[k].start()
     send_og.start()
+    rank_rows(FAR)
     for k in range(PIECES):
         pass_last[k].wait_recv()
     project(NEAR_FAR, False)
@@ -573,6 +596,7 @@
     attended_mine = jnp.concatenate([att_t[:, 0:128], att_t[:, 256:384]], axis=1).T
     token_rows = jnp.concatenate([tok[0:128, :], tok[256:384, :]], axis=0).astype(F32)
     branch = dot(attended_mine.astype(BF16), w_out[pl.ds(half, 384), :])
+    rank_rows(NEAR_FAR)
     swap_att.wait_recv()
     branch = branch + dot(att_recv[...], w_out[pl.ds(other_half, 384), :]) + shifts[2:3, :]
     normed_one, inverse_one = norm(token_rows + branch)
@@ -638,32 +662,41 @@
     spread(SIB, ga_recv[0:128, :].astype(F32))
     spread(SIB_FAR, ga_recv[128:256, :].astype(F32))
 
-    def backward(first, group_at, from_head, to_head):
+    def backward(first, group_at, first_query, count, heads=range(6)):
         rows = slice(128 * first, 128 * first + 256)
+        queries = slice(first_query, first_query + count)
 
         def value_dots(h):
-            return dot(val[h // 2, rows, :], go_t[h])
-
-        grad_prob = value_dots(from_head)
-        for h in range(from_head, to_head):
-            following = value_dots(h + 1) if h + 1 < to_head else None
-            weight = probs[h, rows, :].astype(F32) * share[group_at, h]
-            grad_score = (weight * (grad_prob - delta[h])).astype(BF16)
-            value_part = dot(weight.astype(BF16), go_m[h])
-            key_part = dot(grad_score, q_ext[h, :, 0:128])
+            return dot(val[h // 2, rows, :], go_t[h, :, queries])
+
+        grad_prob = value_dots(heads[0])
+        for h in heads:
+            following = value_dots(h + 1) if h + 1 in heads else None
+            weight = probs[h, rows, queries].astype(F32) * share[group_at, h, :, queries]
+            grad_score = (weight * (grad_prob - delta[h, :, queries])).astype(BF16)
+            value_part = dot(weight.astype(BF16), go_m[h, queries, :])
+            key_part = dot(grad_score, q_ext[h, queries, 0:128])
             rows_h = slice(64 * h, 64 * h + 64)
             query_part = dot(k_t[rows_h, rows], grad_score)
             if first == NEAR_FAR:
-                dq_t[rows_h, :] = query_part
+                dq_t[rows_h, queries] = query_part
             else:
-                dq_t[rows_h, :] += query_part
+                dq_t[rows_h, queries] += query_part
             if h % 2 == 0:
                 grad_values, grad_keys = value_part, key_part
             else:
+                grad_values, grad_keys = grad_values + value_part, grad_keys + key_part
                 cols = slice(64 * h - 64, 64 * h + 64)
                 value_cols = slice(64 * h + 320, 64 * h + 448)
-                d_kv[rows, cols] = (grad_keys + key_part).astype(BF16)
-                d_kv[rows, value_cols] = (grad_values + value_part).astype(BF16)
+                if count == 512:
+                    d_kv[rows, cols] = grad_keys.astype(BF16)
+                    d_kv[rows, value_cols] = grad_values.astype(BF16)
+                elif first_query == 256:
+                    d_held[:, cols] = grad_keys
+                    d_held[:, value_cols] = grad_values
+                else:
+                    d_kv[rows, cols] = (d_held[:, cols] + grad_keys).astype(BF16)
+                    d_kv[rows, value_cols] = (d_held[:, value_cols] + grad_values).astype(BF16)
             grad_prob = following
 
     def token_terms(start):
@@ -692,20 +725,19 @@
         tn_send[128 * k : 128 * k + 128, :] = shared(k).astype(BF16)
         send_parts[k].start()
 
-    backward(NEAR_FAR, PART_LAST, 0, 6)
+    backward(NEAR_FAR, PART_LAST, 0, 512)
     share_out(0, token_terms(128 * NEAR_FAR))
-    backward(NEAR, PART_OWN, 0, 2)
+    backward(NEAR, PART_OWN, 0, 512, range(0, 4))
     pass_on(0)
-    backward(NEAR, PART_OWN, 2, 6)
+    backward(NEAR, PART_OWN, 0, 512, range(4, 6))
     share_out(1, token_terms(128 * NEAR))
-    backward(FAR, PART_FAR, 0, 2)
+    backward(FAR, PART_FAR, 0, 512)
     pass_on(1)
-    backward(FAR, PART_FAR, 2, 6)
     far_terms[...] = token_terms(128 * FAR)
-    backward(OWN, PART_OWN, 0, 6)
-
-    low_dq = (dq_t[...] * 0.125).T.astype(BF16)
-    share_out(2, far_terms[...] + dot_nt(low_dq[256:512, :], w_all[:, 0:384]))
+    backward(OWN, PART_OWN, 256, 256)
+    low_dq_far = (dq_t[:, 256:512] * 0.125).T.astype(BF16)
+    share_out(2, far_terms[...] + dot_nt(low_dq_far, w_all[:, 0:384]))
+    backward(OWN, PART_OWN, 0, 256)
     far_part = shared(2) + g_one[128:256, :]
     send_parts[0].wait_recv()
     ig_buf[128:256, :] = (far_part + tn_recv[0:128, :].astype(F32)).astype(BF16)
@@ -714,17 +746,23 @@
     send_ig.start()
 
     low_dq_t = (dq_t[...] * 0.125).astype(BF16)
-    grad_q_map = dot(low_dq_t, tok[0:512, :]).astype(BF16)
-    grad_v_map = dot(d_kv[:, 384:768].astype(F32).T.astype(BF16), tok[...]).astype(BF16)
-    sum_buf[0:8, :] = jnp.zeros((8, 1024), F32)
-    for row, grad_map in ((0, grad_q_map), (1, grad_v_map)):
-        product_map = dot(grad_map, v_in[...]) * v_out_t[...].astype(F32)
+    low_dv_t = d_kv[:, 384:768].astype(F32).T.astype(BF16)
+    rank_parts, out_parts = [], []
+    for row, product_map in (
+        (0, dot(low_dq_t, rank_in[0:512, :])),
+        (1, dot(low_dv_t, rank_in[...])),
+    ):
+        product_map = product_map * v_out_t[...].astype(F32)
         out_row = out_scale[pl.ds(row, 1), pl.ds(half, 384)]
         out_col = jnp.broadcast_to(out_row, (128, 384)).T[:, 0:1]
-        sum_buf[row : row + 1, :] = jnp.sum(product_map * out_col, axis=0, keepdims=True)
+        rank_part = jnp.sum(product_map * out_col, axis=0, keepdims=True)
+        rank_parts += [rank_part[:, 0:512], rank_part[:, 512:1024]]
         out_part = jnp.sum(product_map * rank_scale[pl.ds(row, 1), :], axis=1, keepdims=True)
-        out_part_row = jnp.broadcast_to(out_part, (384, 128)).T[0:1, :]
-        sum_buf[2 + row : 3 + row, pl.ds(half, 384)] = out_part_row
+        out_part = jnp.broadcast_to(out_part, (384, 128)).T[0:1, :]
+        out_part = jnp.concatenate([out_part, jnp.zeros((1, 128), F32)], axis=1)
+        out_parts += [jnp.where(core == 0, out_part, 0.0), jnp.where(core == 1, out_part, 0.0)]
+    for k, part in enumerate(rank_parts + out_parts):
+        sum_buf[k : k + 1, :] = part
 
     def exchange(k, stage, wheres):
         swaps = [
@@ -744,18 +782,19 @@
         return sum_recv[8 * k : 8 * k + 8, :]
 
     core_swaps = exchange(27, 0, (to_sib,))
-    share_out(3, token_terms(128 * OWN) + dot_nt(low_dq[0:256, :], w_all[:, 0:384]))
+    low_dq = (dq_t[:, 0:256] * 0.125).T.astype(BF16)
+    share_out(3, token_terms(128 * OWN) + dot_nt(low_dq, w_all[:, 0:384]))
     core_swaps[0].wait_recv()
     sum_buf[8:16, :] = sum_buf[0:8, :] + received(0)
     plane_swaps = exchange(28, 1, (to_bx, to_by, to_bxy))
     own_part = shared(3) + g_one[0:128, :]
-    send_parts[1].wait_recv()
-    ig_buf[0:128, :] = (own_part + tn_recv[128:256, :].astype(F32)).astype(BF16)
-    keep_ig.start()
     for swap in plane_swaps:
         swap.wait_recv()
     sum_buf[16:24, :] = (sum_buf[8:16, :] + received(1)) + (received(2) + received(3))
     line_swaps = exchange(31, 2, (to_near, to_far, to_near_far))
+    send_parts[1].wait_recv()
+    ig_buf[0:128, :] = (own_part + tn_recv[128:256, :].astype(F32)).astype(BF16)
+    keep_ig.start()
     for swap in line_swaps:
         swap.wait_recv()
     sums[...] = (sum_buf[16:24, :] + received(4)) + (received(5) + received(6))
@@ -789,12 +828,15 @@
 def finish_kernel(layer_in, grad_in, sums, layer_out, in_grad, rank_total, out_total, norms):
     layer_out[...] = layer_in[...]
     in_grad[...] = grad_in[...]
-    rank_total[...] = sums[0:2, :]
-    out_total[...] = sums[2:4, 0:768]
-    totals = sums[0:4, :]
-    lengths = jnp.sqrt(jnp.sum(totals * totals, axis=1, keepdims=True))
-    for k in range(4):
-        norms[k] = lengths[k, 0]
+    rank_rows = [jnp.concatenate([sums[k : k + 1], sums[k + 1 : k + 2]], axis=1) for k in (0, 2)]
+    out_rows = [
+        jnp.concatenate([sums[k : k + 1, 0:384], sums[k + 1 : k + 2, 0:384]], axis=1) for k in (4, 6)
+    ]
+    for k in range(2):
+        rank_total[k : k + 1, :] = rank_rows[k]
+        out_total[k : k + 1, :] = out_rows[k]
+    for k, row in enumerate(rank_rows + out_rows):
+        norms[k] = jnp.sqrt(jnp.sum(row * row, axis=1, keepdims=True))[0, 0]
 
 
 def fast_body(
@@ -817,6 +859,7 @@
     vmem = pl.BlockSpec(memory_space=pltpu.VMEM)
     smem = pl.BlockSpec(memory_space=pltpu.SMEM)
     shape = tokens.shape
+    small = (rank_scale, out_scale, gains, shifts, ffn_bias.reshape(1, -1))
     scratch = [
         ((1024, 768), BF16),
         ((256, 768), BF16),
@@ -827,6 +870,7 @@
         ((768, 1024), BF16),
         ((1024, 384), BF16),
         ((384, 1024), BF16),
+        ((1024, 1024), BF16),
         ((3, 1024, 256), BF16),
         ((6, 512, 256), BF16),
         ((3, 1024, 128), BF16),
@@ -856,6 +900,7 @@
         ((6, 512, 128), BF16),
         ((6, 1, 512), F32),
         ((1024, 768), BF16),
+        ((256, 768), F32),
         ((384, 512), F32),
         ((512, 768), BF16),
         ((512, 768), BF16),
@@ -864,20 +909,22 @@
         ((256, 768), BF16),
         ((256, 768), BF16),
         ((256, 768), BF16),
-        ((24, 1024), F32),
-        ((56, 1024), F32),
+        ((24, 512), F32),
+        ((56, 512), F32),
     ]
     rows_type = jax.ShapeDtypeStruct(shape, BF16)
     layer_rows, grad_rows, sums = pl.pallas_call(
         layer_kernel,
-        out_shape=(rows_type, rows_type, jax.ShapeDtypeStruct((8, 1024), F32)),
-        in_specs=[hbm] * 8 + [vmem] * 5 + [smem],
+        out_shape=(rows_type, rows_type, jax.ShapeDtypeStruct((8, 512), F32)),
+        in_specs=[hbm] * 14,
         out_specs=(hbm, hbm, vmem),
-        scratch_shapes=[pltpu.VMEM(dims, kind) for dims, kind in scratch]
+        scratch_shapes=[pltpu.VMEM(item.shape, F32) for item in small]
+        + [pltpu.SMEM(splits.shape, jnp.int32)]
+        + [pltpu.VMEM(dims, kind) for dims, kind in scratch]
         + [
             pltpu.SemaphoreType.DMA((34,)),
             pltpu.SemaphoreType.DMA((34,)),
-            pltpu.SemaphoreType.DMA((12,)),
+            pltpu.SemaphoreType.DMA((18,)),
         ],
         compiler_params=pltpu.CompilerParams(
             collective_id=0, has_side_effects=True, vmem_limit_bytes=60 * 2**20
@@ -892,11 +939,7 @@
         vera_in,
         vera_out,
         out_grad,
-        rank_scale,
-        out_scale,
-        gains,
-        shifts,
-        ffn_bias.reshape(1, -1),
+        *small,
         splits,
     )
     return pl.pallas_call(

time: 67.3 us -> 64.1 us (0.952)
  Pallas kernels: 66.3 us -> 63.2 us
    pallas_call x1, Pallas kernels: 64.2 us -> 61.1 us  [fast_body(): pl.pallas_call(layer_kernel, out_shape=(rows_type, rows_type, jax.ShapeDt...]
where the time goes in v4:
time: 64.1 us; the launch traced here: 64 us
  Pallas kernels  63.2 us (99%)
  between operations  0.83 us (1%)
    pallas_call x1, Pallas kernels, fast_body(): pl.pallas_call(layer_kernel, out_shape=(rows_type, rows_type, jax.ShapeDt...  61.1 us
    pallas_call x1, Pallas kernels, fast_body(): pl.pallas_call(finish_kernel, out_shape=(rows_type, rows_type, jax.ShapeD...  2.05 us

profile of v4, /device:TPU:0, one launch (start us, length us, event | category | flops | bytes accessed | tf_op | source)
XLA Modules:
  0.0 64.0 jit_solution(2595355189093107715)
XLA Ops:
  0.6 61.1 %encoder_layer.1 = (bf16[2,128,768]{2,1,0:T(8,128)(2,1)}, bf16[2,128,768]{2,1,0:T(8,128)(2,1)}, f32[8,512]{1,0:T(8,128)}) custom-call(bf16[2,128,768]{2,1,0:T(8,128)(2,1)} %tokens.1, bf16[768,2304]{1,0:T(8,128)(2,1)} %attn_in.1, bf16[768,768]{1,0:T(8,128)(2,1)} %out_w.1, bf16[768,3072]{1,0:T(8,128)(2,1)} %ffn_in.1, bf16[3072,768]{1,0:T(8,128)(2,1)} %ffn_out.1, ...), custom_call_target="tpu_custom_call" | custom-call | tf_op jit(solution)/shard_map/encoder_layer/pallas_call | solution.py:916
  61.8 2.1 %finish.1 = (bf16[2,128,768]{2,1,0:T(8,128)(2,1)}, bf16[2,128,768]{2,1,0:T(8,128)(2,1)}, f32[2,1024]{1,0:T(2,128)}, f32[2,768]{1,0:T(2,128)}, f32[4]{0:T(128)}) custom-call(bf16[2,128,768]{2,1,0:T(8,128)(2,1)} %get-tuple-element.8.layer_in, bf16[2,128,768]{2,1,0:T(8,128)(2,1)} %get-tuple-element.9.grad_in, f32[8,512]{1,0:T(8,128)} %get-tuple-element.10.sums), custom_call_target="tpu_custom_call" | custom-call | tf_op jit(solution)/shard_map/finish/pallas_call | solution.py:945

commit v5 on v4

--- a/solution.py
+++ b/solution.py
@@ -259,7 +259,6 @@
 
 OWN, SIB, FAR, SIB_FAR, NEAR_FAR, SIB_NEAR_FAR, NEAR, SIB_NEAR = range(8)
 PIECES = 2
-PART_OWN, PART_FAR, PART_LAST = range(3)
 
 
 def layer_kernel(
@@ -313,7 +312,6 @@
     hid,
     n_one,
     wide,
-    gprime,
     low_rows,
     g_two,
     g_one,
@@ -326,7 +324,6 @@
     delta,
     d_kv,
     d_held,
-    dq_t,
     part_send,
     part_recv,
     part_mine,
@@ -417,10 +414,16 @@
     pass_far_sib = remote(14, block(tok, FAR), block(tok, SIB_FAR), to_sib)
     pass_near_sib = remote(15, block(tok, NEAR), block(tok, SIB_NEAR), to_sib)
     send_og = remote(16, out_grad.at[1 - group], og.at[pl.ds(128, 128)], to_far)
-    send_near.start()
+    outer = (s // 2) % 2 == group
+    inner = jnp.logical_not(outer)
+
+    def start_far():
+        for item in send_far:
+            item.start()
+
+    pl.when(outer)(start_far)
+    pl.when(inner)(send_near.start)
     send_sib.start()
-    for item in send_far:
-        item.start()
 
     for item in (*small_loads, *loads[1:6]):
         item.wait()
@@ -464,6 +467,9 @@
             ).astype(BF16)
             for h in range(6):
                 q_ext[h, 128 * k : 128 * k + 128, 128:256] = query_side
+
+    pl.when(inner)(start_far)
+    pl.when(outer)(send_near.start)
 
     shift_q = shifts[0:1, pl.ds(half, 384)]
     shift_v = shifts[1:2, pl.ds(half, 384)]
@@ -490,8 +496,10 @@
                 masked = jnp.where(mine, low_query[:, 128 * p : 128 * p + 128], 0.0)
                 q_ext[h, to, 0:128] = masked.astype(BF16)
 
-    def attend(group_at, starts_at, first_query, count):
+    def attend(blocks, first_query, count):
         queries = slice(first_query, first_query + count)
+        part_at = blocks[0] // 2
+        starts_at = [128 * first for first in blocks]
         peaks, totals, outs = {}, {}, {}
 
         def scores(h, at):
@@ -516,63 +524,97 @@
                 if h < 5:
                     scores(h + 1, at)
                 weights(h, at)
-            part_top[group_at, h, :, queries] = peaks[h]
-            part_sum[group_at, h, :, queries] = totals[h]
-            part_out[group_at, 64 * h : 64 * h + 64, queries] = outs[h]
+            part_top[part_at, h, :, queries] = peaks[h]
+            part_sum[part_at, h, :, queries] = totals[h]
+            part_out[part_at, 64 * h : 64 * h + 64, queries] = outs[h]
 
     def combine(first_query, groups):
         queries = slice(first_query, first_query + 256)
         for h in range(6):
             rows_h = slice(64 * h, 64 * h + 64)
-            tops = [part_top[g, h, :, queries] for g in groups]
+            parts = [group_of[0] // 2 for group_of in groups]
+            tops = [part_top[k, h, :, queries] for k in parts]
             top = functools.reduce(jnp.maximum, tops)
             shares = [jnp.exp(one - top) for one in tops]
             total = functools.reduce(
-                jnp.add, [w * part_sum[g, h, :, queries] for w, g in zip(shares, groups)]
+                jnp.add, [w * part_sum[k, h, :, queries] for w, k in zip(shares, parts)]
             )
             inverse = 1.0 / total
             shares = [w * inverse for w in shares]
             att_t[rows_h, queries] = functools.reduce(
-                jnp.add, [w * part_out[g, rows_h, queries] for w, g in zip(shares, groups)]
+                jnp.add, [w * part_out[k, rows_h, queries] for w, k in zip(shares, parts)]
             )
-            for w, g in zip(shares, groups):
-                share[g, h, :, queries] = w
-            if len(groups) == 2:
-                share[PART_FAR, h, :, queries] = shares[0]
+            for w, group_of in zip(shares, groups):
+                for first in group_of:
+                    share[first // 2, h, :, queries] = w
 
     def rank_rows(first):
         to = slice(128 * first, 128 * first + 256)
         rank_in[to, :] = dot(tok[to, :], v_in[...]).astype(BF16)
+
+    def pass_far():
+        for k in range(PIECES):
+            send_far[k].wait_recv()
+            pass_far_near[k].start()
+        pass_far_sib.start()
+
+    def near_blocks():
+        send_near.wait_recv()
+        pass_near_sib.start()
+        pass_near_sib.wait_recv()
+        project(NEAR, False)
+
+    def far_blocks():
+        pass_far_sib.wait_recv()
+        project(FAR, True)
+
+    def pass_last_on():
+        for k in range(PIECES):
+            pass_far_near[k].wait_recv()
+            pass_last[k].start()
+
+    def last_blocks():
+        for k in range(PIECES):
+            pass_last[k].wait_recv()
+        project(NEAR_FAR, False)
 
     loads[0].wait()
     send_sib.wait_recv()
     project(OWN, True)
     rank_rows(OWN)
-    send_near.wait_recv()
-    pass_near_sib.start()
-    pass_near_sib.wait_recv()
-    project(NEAR, False)
-    rank_rows(NEAR)
-    for k in range(PIECES):
-        send_far[k].wait_recv()
-        pass_far_near[k].start()
-    pass_far_sib.start()
-    attend(PART_OWN, (128 * OWN, 128 * NEAR), 0, 256)
-    pass_far_sib.wait_recv()
-    project(FAR, True)
-    attend(PART_FAR, (128 * FAR,), 0, 256)
-    attend(PART_OWN, (128 * OWN, 128 * NEAR, 128 * FAR), 256, 256)
-    for k in range(PIECES):
-        pass_far_near[k].wait_recv()
-        pass_last[k].start()
-    send_og.start()
-    rank_rows(FAR)
-    for k in range(PIECES):
-        pass_last[k].wait_recv()
-    project(NEAR_FAR, False)
-    attend(PART_LAST, (128 * NEAR_FAR,), 0, 512)
-    combine(0, (PART_OWN, PART_FAR, PART_LAST))
-    combine(256, (PART_OWN, PART_LAST))
+    attend((OWN,), 0, 256)
+
+    @pl.when(inner)
+    def _():
+        pass_far()
+        far_blocks()
+        attend((FAR,), 0, 256)
+        attend((OWN, FAR), 256, 256)
+        near_blocks()
+        attend((NEAR,), 0, 512)
+        rank_rows(NEAR)
+        pass_last_on()
+        send_og.start()
+        last_blocks()
+        attend((NEAR_FAR,), 0, 512)
+        combine(0, ((OWN,), (FAR,), (NEAR,), (NEAR_FAR,)))
+        combine(256, ((OWN, FAR), (NEAR,), (NEAR_FAR,)))
+
+    @pl.when(outer)
+    def _():
+        near_blocks()
+        attend((NEAR,), 0, 256)
+        pass_far()
+        rank_rows(NEAR)
+        far_blocks()
+        attend((FAR,), 0, 256)
+        attend((OWN, FAR, NEAR), 256, 256)
+        pass_last_on()
+        send_og.start()
+        last_blocks()
+        attend((NEAR_FAR,), 0, 512)
+        combine(0, ((OWN,), (FAR,), (NEAR,), (NEAR_FAR,)))
+        combine(256, ((OWN, FAR, NEAR), (NEAR_FAR,)))
 
     swap_att = remote(17, att_send, att_recv, to_sib)
     for k, at in ((0, 128 * SIB), (128, 128 * SIB_FAR)):
@@ -596,6 +638,7 @@
     attended_mine = jnp.concatenate([att_t[:, 0:128], att_t[:, 256:384]], axis=1).T
     token_rows = jnp.concatenate([tok[0:128, :], tok[256:384, :]], axis=0).astype(F32)
     branch = dot(attended_mine.astype(BF16), w_out[pl.ds(half, 384), :])
+    rank_rows(FAR)
     rank_rows(NEAR_FAR)
     swap_att.wait_recv()
     branch = branch + dot(att_recv[...], w_out[pl.ds(other_half, 384), :]) + shifts[2:3, :]
@@ -607,12 +650,15 @@
 
     loads[7].wait()
     loads[8].wait()
+    def slope(t):
+        return s_buf.at[t // 2048, pl.ds(t % 2048 // 2, 256)]
+
     for t in range(0, 3072, 512):
         cols = slice(t, t + 512)
         inner = dot(low_rows[...], w_one[:, cols]) + ffn_bias[:, cols]
         phi = 0.5 * (1.0 + lax.erf(inner * 0.7071067811865476))
         density = 0.3989422804014327 * jnp.exp(-0.5 * inner * inner)
-        gprime[:, cols] = phi + inner * density
+        slope(t)[...] = phi + inner * density
         wide[:, cols] = (inner * phi).astype(BF16)
     ffn_branch = dot(wide[...], w_two[...])
     normed_two, inverse_two = norm(hid[...] + ffn_branch + shifts[3:4, :])
@@ -629,7 +675,7 @@
     for t in range(0, 3072, 512):
         cols = slice(t, t + 512)
         grad_act = dot_nt(low_rows[...], w_two[cols, :])
-        wide[:, cols] = (grad_act * gprime[:, cols]).astype(BF16)
+        wide[:, cols] = (grad_act * slope(t)[...]).astype(BF16)
     grad_hidden = g_two[...] + dot_nt(wide[...], w_one[...])
     grad_one = norm_back(grad_hidden, n_one[...], inverse_one, gains[0:1, :])
     g_one[...] = grad_one
@@ -662,7 +708,9 @@
     spread(SIB, ga_recv[0:128, :].astype(F32))
     spread(SIB_FAR, ga_recv[128:256, :].astype(F32))
 
-    def backward(first, group_at, first_query, count, heads=range(6)):
+    dq_t = part_out.at[0]
+
+    def backward(first, first_query, count, heads=range(6)):
         rows = slice(128 * first, 128 * first + 256)
         queries = slice(first_query, first_query + count)
 
@@ -672,7 +720,7 @@
         grad_prob = value_dots(heads[0])
         for h in heads:
             following = value_dots(h + 1) if h + 1 in heads else None
-            weight = probs[h, rows, queries].astype(F32) * share[group_at, h, :, queries]
+            weight = probs[h, rows, queries].astype(F32) * share[first // 2, h, :, queries]
             grad_score = (weight * (grad_prob - delta[h, :, queries])).astype(BF16)
             value_part = dot(weight.astype(BF16), go_m[h, queries, :])
             key_part = dot(grad_score, q_ext[h, queries, 0:128])
@@ -725,19 +773,19 @@
         tn_send[128 * k : 128 * k + 128, :] = shared(k).astype(BF16)
         send_parts[k].start()
 
-    backward(NEAR_FAR, PART_LAST, 0, 512)
+    backward(NEAR_FAR, 0, 512)
     share_out(0, token_terms(128 * NEAR_FAR))
-    backward(NEAR, PART_OWN, 0, 512, range(0, 4))
+    backward(NEAR, 0, 512, range(0, 4))
     pass_on(0)
-    backward(NEAR, PART_OWN, 0, 512, range(4, 6))
+    backward(NEAR, 0, 512, range(4, 6))
     share_out(1, token_terms(128 * NEAR))
-    backward(FAR, PART_FAR, 0, 512)
+    backward(FAR, 0, 512)
     pass_on(1)
     far_terms[...] = token_terms(128 * FAR)
-    backward(OWN, PART_OWN, 256, 256)
+    backward(OWN, 256, 256)
     low_dq_far = (dq_t[:, 256:512] * 0.125).T.astype(BF16)
     share_out(2, far_terms[...] + dot_nt(low_dq_far, w_all[:, 0:384]))
-    backward(OWN, PART_OWN, 0, 256)
+    backward(OWN, 0, 256)
     far_part = shared(2) + g_one[128:256, :]
     send_parts[0].wait_recv()
     ig_buf[128:256, :] = (far_part + tn_recv[0:128, :].astype(F32)).astype(BF16)
@@ -879,16 +927,15 @@
         ((6, 1024, 512), BF16),
         ((2, 1024, 512), F32),
         ((384, 512), F32),
-        ((3, 6, 1, 512), F32),
-        ((3, 6, 1, 512), F32),
-        ((3, 384, 512), F32),
-        ((3, 6, 1, 512), F32),
+        ((4, 6, 1, 512), F32),
+        ((4, 6, 1, 512), F32),
+        ((4, 384, 512), F32),
+        ((4, 6, 1, 512), F32),
         ((256, 384), BF16),
         ((256, 384), BF16),
         ((256, 768), F32),
         ((256, 768), F32),
         ((256, 3072), BF16),
-        ((256, 3072), F32),
         ((256, 768), BF16),
         ((256, 768), F32),
         ((256, 768), F32),
@@ -901,7 +948,6 @@
         ((6, 1, 512), F32),
         ((1024, 768), BF16),
         ((256, 768), F32),
-        ((384, 512), F32),
         ((512, 768), BF16),
         ((512, 768), BF16),
         ((512, 768), F32),
@@ -913,11 +959,12 @@
         ((56, 512), F32),
     ]
     rows_type = jax.ShapeDtypeStruct(shape, BF16)
+    held_rows = pltpu.VMEM(shape, BF16)
     layer_rows, grad_rows, sums = pl.pallas_call(
         layer_kernel,
-        out_shape=(rows_type, rows_type, jax.ShapeDtypeStruct((8, 512), F32)),
+        out_shape=(held_rows, held_rows, pltpu.VMEM((8, 512), F32)),
         in_specs=[hbm] * 14,
-        out_specs=(hbm, hbm, vmem),
+        out_specs=(vmem, vmem, vmem),
         scratch_shapes=[pltpu.VMEM(item.shape, F32) for item in small]
         + [pltpu.SMEM(splits.shape, jnp.int32)]
         + [pltpu.VMEM(dims, kind) for dims, kind in scratch]
@@ -954,7 +1001,7 @@
         in_specs=[vmem, vmem, vmem],
         out_specs=(vmem, vmem, vmem, vmem, smem),
         name="finish",
-    )(layer_rows, grad_rows, sums)
+    )(*[pltpu.with_memory_space_constraint(x, pltpu.VMEM) for x in (layer_rows, grad_rows, sums)])
 
 
 def solution(mesh):

time: 64.1 us -> 60.1 us (0.938)
  Pallas kernels: 63.2 us -> 59.1 us
    pallas_call x1, Pallas kernels: 61.1 us -> 58.1 us  [fast_body(): pl.pallas_call(layer_kernel, out_shape=(held_rows, held_rows, pltpu.VMEM(...]
    pallas_call x1, Pallas kernels: 2.05 us -> 0.93 us  [fast_body(): pl.pallas_call(finish_kernel, out_shape=(rows_type, rows_type, jax.ShapeD...]
where the time goes in v5:
time: 60.1 us; the launch traced here: 59.9 us
  Pallas kernels  59.1 us (98%)
  between operations  0.83 us (1%)
    pallas_call x1, Pallas kernels, fast_body(): pl.pallas_call(layer_kernel, out_shape=(held_rows, held_rows, pltpu.VMEM(...  58.1 us

profile of v5, /device:TPU:0, one launch (start us, length us, event | category | flops | bytes accessed | tf_op | source)
XLA Modules:
  0.0 59.9 jit_solution(7962187090184487434)
XLA Ops:
  0.6 58.1 %encoder_layer.1 = (bf16[2,128,768]{2,1,0:T(8,128)(2,1)S(1)}, bf16[2,128,768]{2,1,0:T(8,128)(2,1)S(1)}, f32[8,512]{1,0:T(8,128)S(1)}) custom-call(bf16[2,128,768]{2,1,0:T(8,128)(2,1)} %tokens.1, bf16[768,2304]{1,0:T(8,128)(2,1)} %attn_in.1, bf16[768,768]{1,0:T(8,128)(2,1)} %out_w.1, bf16[768,3072]{1,0:T(8,128)(2,1)} %ffn_in.1, bf16[3072,768]{1,0:T(8,128)(2,1)} %ffn_out.1, ...), custom_call_target="tpu_custom_call" | custom-call | tf_op jit(solution)/shard_map/encoder_layer/pallas_call | solution.py:963
  58.8 0.9 %finish.1 = (bf16[2,128,768]{2,1,0:T(8,128)(2,1)}, bf16[2,128,768]{2,1,0:T(8,128)(2,1)}, f32[2,1024]{1,0:T(2,128)}, f32[2,768]{1,0:T(2,128)}, f32[4]{0:T(128)}) custom-call(bf16[2,128,768]{2,1,0:T(8,128)(2,1)S(1)} %get-tuple-element.8.layer_in, bf16[2,128,768]{2,1,0:T(8,128)(2,1)S(1)} %get-tuple-element.9.grad_in, f32[8,512]{1,0:T(8,128)S(1)} %get-tuple-element.10.sums), custom_call_target="tpu_custom_call" | custom-call | tf_op jit(solution)/shard_map/finish/pallas_call | solution.py:992

commit v6 on v5

--- a/solution.py
+++ b/solution.py
@@ -258,7 +258,7 @@
 
 
 OWN, SIB, FAR, SIB_FAR, NEAR_FAR, SIB_NEAR_FAR, NEAR, SIB_NEAR = range(8)
-PIECES = 2
+PIECES = 4
 
 
 def layer_kernel(
@@ -394,7 +394,7 @@
         local(16, ffn_bias_in, ffn_bias),
         local(17, splits_in, splits),
     ]
-    for item in (*small_loads, *loads):
+    for item in (*loads[1:6], *small_loads, loads[0]):
         item.start()
     pl.semaphore_wait(barrier, 7)
 
@@ -427,6 +427,8 @@
 
     for item in (*small_loads, *loads[1:6]):
         item.wait()
+    for item in loads[6:10]:
+        item.start()
     for row, at in ((0, 0), (1, 768)):
         scale_row = rank_scale[pl.ds(row, 1), :]
         out_row = out_scale[pl.ds(row, 1), pl.ds(half, 384)]
@@ -475,8 +477,8 @@
     shift_v = shifts[1:2, pl.ds(half, 384)]
     low_lane = lax.broadcasted_iota(jnp.int32, (256, 128), 1) < 64
 
-    def project(first, queries):
-        to = slice(128 * first, 128 * first + 256)
+    def project(first, queries, count=256):
+        to = slice(128 * first, 128 * first + count)
         rows = tok[to, :]
         keys = dot(rows, w_all[:, 384:768])
         values = dot(rows, w_all[:, 768:1152]) + shift_v
@@ -574,9 +576,10 @@
             pass_last[k].start()
 
     def last_blocks():
+        project(NEAR_FAR, False, 128)
         for k in range(PIECES):
             pass_last[k].wait_recv()
-        project(NEAR_FAR, False)
+        project(SIB_NEAR_FAR, False, 128)
 
     loads[0].wait()
     send_sib.wait_recv()
@@ -662,11 +665,11 @@
         wide[:, cols] = (inner * phi).astype(BF16)
     ffn_branch = dot(wide[...], w_two[...])
     normed_two, inverse_two = norm(hid[...] + ffn_branch + shifts[3:4, :])
-    lo_buf[...] = (normed_two * gains[1:2, :] + shifts[5:6, :]).astype(BF16)
-    send_lo = remote(18, lo_buf.at[pl.ds(128, 128)], layer_out.at[group], to_far)
-    keep_lo = local(10, lo_buf.at[pl.ds(0, 128)], layer_out.at[group])
+    out_rows = (normed_two * gains[1:2, :] + shifts[5:6, :]).astype(BF16)
+    lo_buf[...] = out_rows[128:256]
+    send_lo = remote(18, lo_buf, layer_out.at[group], to_far)
     send_lo.start()
-    keep_lo.start()
+    layer_out[group] = out_rows[0:128]
     loads[9].wait()
     send_og.wait_recv()
     grad_two = norm_back(og[...].astype(F32), normed_two, inverse_two, gains[1:2, :])
@@ -775,9 +778,9 @@
 
     backward(NEAR_FAR, 0, 512)
     share_out(0, token_terms(128 * NEAR_FAR))
-    backward(NEAR, 0, 512, range(0, 4))
+    backward(NEAR, 0, 512, range(0, 2))
     pass_on(0)
-    backward(NEAR, 0, 512, range(4, 6))
+    backward(NEAR, 0, 512, range(2, 6))
     share_out(1, token_terms(128 * NEAR))
     backward(FAR, 0, 512)
     pass_on(1)
@@ -788,9 +791,8 @@
     backward(OWN, 0, 256)
     far_part = shared(2) + g_one[128:256, :]
     send_parts[0].wait_recv()
-    ig_buf[128:256, :] = (far_part + tn_recv[0:128, :].astype(F32)).astype(BF16)
-    send_ig = remote(26, ig_buf.at[pl.ds(128, 128)], in_grad.at[group], to_far)
-    keep_ig = local(11, ig_buf.at[pl.ds(0, 128)], in_grad.at[group])
+    ig_buf[...] = (far_part + tn_recv[0:128, :].astype(F32)).astype(BF16)
+    send_ig = remote(26, ig_buf, in_grad.at[group], to_far)
     send_ig.start()
 
     low_dq_t = (dq_t[...] * 0.125).astype(BF16)
@@ -841,16 +843,13 @@
     sum_buf[16:24, :] = (sum_buf[8:16, :] + received(1)) + (received(2) + received(3))
     line_swaps = exchange(31, 2, (to_near, to_far, to_near_far))
     send_parts[1].wait_recv()
-    ig_buf[0:128, :] = (own_part + tn_recv[128:256, :].astype(F32)).astype(BF16)
-    keep_ig.start()
+    in_grad[group] = (own_part + tn_recv[128:256, :].astype(F32)).astype(BF16)
     for swap in line_swaps:
         swap.wait_recv()
     sums[...] = (sum_buf[16:24, :] + received(4)) + (received(5) + received(6))
 
     send_lo.wait_recv()
     send_ig.wait_recv()
-    keep_lo.wait()
-    keep_ig.wait()
     for item in (
         *send_far,
         *pass_far_near,
@@ -939,7 +938,7 @@
         ((256, 768), BF16),
         ((256, 768), F32),
         ((256, 768), F32),
-        ((256, 768), BF16),
+        ((128, 768), BF16),
         ((256, 384), BF16),
         ((256, 384), BF16),
         ((256, 384), BF16),
@@ -954,7 +953,7 @@
         ((256, 768), F32),
         ((256, 768), BF16),
         ((256, 768), BF16),
-        ((256, 768), BF16),
+        ((128, 768), BF16),
         ((24, 512), F32),
         ((56, 512), F32),
     ]

time: 60.1 us -> 59.2 us (0.985)
  Pallas kernels: 59.1 us -> 58.2 us
    pallas_call x1, Pallas kernels: 58.1 us -> 57.3 us  [fast_body(): pl.pallas_call(layer_kernel, out_shape=(held_rows, held_rows, pltpu.VMEM(...]
where the time goes in v6:
time: 59.2 us; the launch traced here: 59 us
  Pallas kernels  58.2 us (98%)
  between operations  0.85 us (1%)
    pallas_call x1, Pallas kernels, fast_body(): pl.pallas_call(layer_kernel, out_shape=(held_rows, held_rows, pltpu.VMEM(...  57.3 us

profile of v6, /device:TPU:0, one launch (start us, length us, event | category | flops | bytes accessed | tf_op | source)
XLA Modules:
  0.0 59.0 jit_solution(8596372703626177461)
XLA Ops:
  0.6 57.3 %encoder_layer.1 = (bf16[2,128,768]{2,1,0:T(8,128)(2,1)S(1)}, bf16[2,128,768]{2,1,0:T(8,128)(2,1)S(1)}, f32[8,512]{1,0:T(8,128)S(1)}) custom-call(bf16[2,128,768]{2,1,0:T(8,128)(2,1)} %tokens.1, bf16[768,2304]{1,0:T(8,128)(2,1)} %attn_in.1, bf16[768,768]{1,0:T(8,128)(2,1)} %out_w.1, bf16[768,3072]{1,0:T(8,128)(2,1)} %ffn_in.1, bf16[3072,768]{1,0:T(8,128)(2,1)} %ffn_out.1, ...), custom_call_target="tpu_custom_call" | custom-call | tf_op jit(solution)/shard_map/encoder_layer/pallas_call | solution.py:962
  57.9 0.9 %finish.1 = (bf16[2,128,768]{2,1,0:T(8,128)(2,1)}, bf16[2,128,768]{2,1,0:T(8,128)(2,1)}, f32[2,1024]{1,0:T(2,128)}, f32[2,768]{1,0:T(2,128)}, f32[4]{0:T(128)}) custom-call(bf16[2,128,768]{2,1,0:T(8,128)(2,1)S(1)} %get-tuple-element.8.layer_in, bf16[2,128,768]{2,1,0:T(8,128)(2,1)S(1)} %get-tuple-element.9.grad_in, f32[8,512]{1,0:T(8,128)S(1)} %get-tuple-element.10.sums), custom_call_target="tpu_custom_call" | custom-call | tf_op jit(solution)/shard_map/finish/pallas_call | solution.py:991

commit v7 on v6

--- a/solution.py
+++ b/solution.py
@@ -470,7 +470,6 @@
             for h in range(6):
                 q_ext[h, 128 * k : 128 * k + 128, 128:256] = query_side
 
-    pl.when(inner)(start_far)
     pl.when(outer)(send_near.start)
 
     shift_q = shifts[0:1, pl.ds(half, 384)]
@@ -480,8 +479,9 @@
     def project(first, queries, count=256):
         to = slice(128 * first, 128 * first + count)
         rows = tok[to, :]
-        keys = dot(rows, w_all[:, 384:768])
-        values = dot(rows, w_all[:, 768:1152]) + shift_v
+        made = dot(rows, w_all[...] if queries else w_all[:, 384:1152])
+        keys = made[:, made.shape[1] - 768 : made.shape[1] - 384]
+        values = made[:, made.shape[1] - 384 :] + shift_v
         low_keys = keys.astype(BF16)
         low_values = values.astype(BF16)
         for p in range(3):
@@ -490,7 +490,7 @@
         k_t[:, to] = keys.T.astype(BF16)
         v_t[:, to] = values.T.astype(BF16)
         if queries:
-            query = dot(rows, w_all[:, 0:384]) + shift_q
+            query = made[:, 0:384] + shift_q
             low_query = query.astype(BF16).astype(F32) * 0.125
             for h in range(6):
                 p = h // 2
@@ -585,6 +585,7 @@
     send_sib.wait_recv()
     project(OWN, True)
     rank_rows(OWN)
+    pl.when(inner)(start_far)
     attend((OWN,), 0, 256)
 
     @pl.when(inner)

time: 59.2 us -> 58.4 us (0.986)
  Pallas kernels: 58.2 us -> 57.4 us
    pallas_call x1, Pallas kernels: 57.3 us -> 56.5 us  [fast_body(): pl.pallas_call(layer_kernel, out_shape=(held_rows, held_rows, pltpu.VMEM(...]
where the time goes in v7:
time: 58.4 us; the launch traced here: 58.2 us
  Pallas kernels  57.4 us (98%)
  between operations  0.85 us (1%)
    pallas_call x1, Pallas kernels, fast_body(): pl.pallas_call(layer_kernel, out_shape=(held_rows, held_rows, pltpu.VMEM(...  56.5 us

profile of v7, /device:TPU:0, one launch (start us, length us, event | category | flops | bytes accessed | tf_op | source)
XLA Modules:
  0.0 58.2 jit_solution(4756439648423887932)
XLA Ops:
  0.6 56.5 %encoder_layer.1 = (bf16[2,128,768]{2,1,0:T(8,128)(2,1)S(1)}, bf16[2,128,768]{2,1,0:T(8,128)(2,1)S(1)}, f32[8,512]{1,0:T(8,128)S(1)}) custom-call(bf16[2,128,768]{2,1,0:T(8,128)(2,1)} %tokens.1, bf16[768,2304]{1,0:T(8,128)(2,1)} %attn_in.1, bf16[768,768]{1,0:T(8,128)(2,1)} %out_w.1, bf16[768,3072]{1,0:T(8,128)(2,1)} %ffn_in.1, bf16[3072,768]{1,0:T(8,128)(2,1)} %ffn_out.1, ...), custom_call_target="tpu_custom_call" | custom-call | tf_op jit(solution)/shard_map/encoder_layer/pallas_call | solution.py:963
  57.1 0.9 %finish.1 = (bf16[2,128,768]{2,1,0:T(8,128)(2,1)}, bf16[2,128,768]{2,1,0:T(8,128)(2,1)}, f32[2,1024]{1,0:T(2,128)}, f32[2,768]{1,0:T(2,128)}, f32[4]{0:T(128)}) custom-call(bf16[2,128,768]{2,1,0:T(8,128)(2,1)S(1)} %get-tuple-element.8.layer_in, bf16[2,128,768]{2,1,0:T(8,128)(2,1)S(1)} %get-tuple-element.9.grad_in, f32[8,512]{1,0:T(8,128)S(1)} %get-tuple-element.10.sums), custom_call_target="tpu_custom_call" | custom-call | tf_op jit(solution)/shard_map/finish/pallas_call | solution.py:992

commit v8 on v7

--- a/solution.py
+++ b/solution.py
@@ -596,9 +596,9 @@
         attend((OWN, FAR), 256, 256)
         near_blocks()
         attend((NEAR,), 0, 512)
+        send_og.start()
         rank_rows(NEAR)
         pass_last_on()
-        send_og.start()
         last_blocks()
         attend((NEAR_FAR,), 0, 512)
         combine(0, ((OWN,), (FAR,), (NEAR,), (NEAR_FAR,)))
@@ -613,8 +613,8 @@
         far_blocks()
         attend((FAR,), 0, 256)
         attend((OWN, FAR, NEAR), 256, 256)
+        send_og.start()
         pass_last_on()
-        send_og.start()
         last_blocks()
         attend((NEAR_FAR,), 0, 512)
         combine(0, ((OWN,), (FAR,), (NEAR,), (NEAR_FAR,)))

time: 58.4 us -> 58 us (level)
  no operation moved by 1% of the time
where the time goes in v8:
time: 58 us; the launch traced here: 57.8 us
  Pallas kernels  57 us (98%)
  between operations  0.85 us (1%)
    pallas_call x1, Pallas kernels, fast_body(): pl.pallas_call(layer_kernel, out_shape=(held_rows, held_rows, pltpu.VMEM(...  56 us

profile of v8, /device:TPU:0, one launch (start us, length us, event | category | flops | bytes accessed | tf_op | source)
XLA Modules:
  0.0 57.8 jit_solution(13464857377016290174)
XLA Ops:
  0.6 56.0 %encoder_layer.1 = (bf16[2,128,768]{2,1,0:T(8,128)(2,1)S(1)}, bf16[2,128,768]{2,1,0:T(8,128)(2,1)S(1)}, f32[8,512]{1,0:T(8,128)S(1)}) custom-call(bf16[2,128,768]{2,1,0:T(8,128)(2,1)} %tokens.1, bf16[768,2304]{1,0:T(8,128)(2,1)} %attn_in.1, bf16[768,768]{1,0:T(8,128)(2,1)} %out_w.1, bf16[768,3072]{1,0:T(8,128)(2,1)} %ffn_in.1, bf16[3072,768]{1,0:T(8,128)(2,1)} %ffn_out.1, ...), custom_call_target="tpu_custom_call" | custom-call | tf_op jit(solution)/shard_map/encoder_layer/pallas_call | solution.py:963
  56.7 0.9 %finish.1 = (bf16[2,128,768]{2,1,0:T(8,128)(2,1)}, bf16[2,128,768]{2,1,0:T(8,128)(2,1)}, f32[2,1024]{1,0:T(2,128)}, f32[2,768]{1,0:T(2,128)}, f32[4]{0:T(128)}) custom-call(bf16[2,128,768]{2,1,0:T(8,128)(2,1)S(1)} %get-tuple-element.8.layer_in, bf16[2,128,768]{2,1,0:T(8,128)(2,1)S(1)} %get-tuple-element.9.grad_in, f32[8,512]{1,0:T(8,128)S(1)} %get-tuple-element.10.sums), custom_call_target="tpu_custom_call" | custom-call | tf_op jit(solution)/shard_map/finish/pallas_call | solution.py:992
